TPU v7x, 256 devices: a whole 4x4x8 slice. The times are simulated.
256 devices in a mesh: region: 8 (over y, x_hi), blk: 32 (over x_lo, z, core).
Axes of the slice: x: 4 (x_hi: 2, x_lo: 2; x = x_hi * 2 + x_lo), y: 4, z: 8, core: 2. Of those that a mesh axis runs over, the one named last changes fastest.
Arguments:
- incident: bfloat16 [8, 8, 256, 32, 128], P(None, 'region', 'blk'), may hold values from -6 to 6
- past_currents: bfloat16 [4, 8, 256, 32, 128], P(None, 'region', 'blk'), may hold values from -6 to 6
- self_inverse: bfloat16 [8, 256, 128, 128], P('region', 'blk'), may hold values from -0.5 to 0.5
- near_tiles: bfloat16 [8, 256, 32, 128, 128], P('region', 'blk'), may hold values from -0.046875 to 0.046875
- near_cols: int32 [8, 256, 32], P('region', 'blk'), may hold values from 0 to 255, as said below
- near_delay: int32 [8, 256, 32], P('region', 'blk'), may hold values from 1 to 4
- block_slot: int32 [8, 256], P('region'), may hold values from 0 to 255, as said below
- far_out: bfloat16 [8, 256, 128, 64], P('region', 'blk'), may hold values from -0.015625 to 0.015625
- far_in: bfloat16 [8, 256, 64, 128], P('region', 'blk'), may hold values from -0.75 to 0.75
- far_pairs: int32 [8, 7], P('region'), may hold values from 0 to 7, as said below
- far_delay: int32 [8, 7], P('region'), may hold values from 1 to 4
- far_coupling: float32 [8, 7, 64, 64], P('region'), may hold values from -0.25 to 0.25
Outputs:
- currents: bfloat16 [8, 8, 256, 32, 128], P(None, 'region', 'blk')
Inputs may be any that keep to these rules, and one draw needn't show every extreme that they name: `block_slot`: each region's ids are a permutation of 0 to 255. `near_cols`: for block row at position b, every near source block is stored on a blk device at most 4 devices from the device of b, and the first tile of every row lies exactly 4 devices away. `far_pairs`: region g lists each of the other 7 regions exactly once.
All inputs are finite; a program needn't handle non-finite values.
Results may differ from a plain program's by a relative error of at most 0.01.
Values may be sent and summed in bfloat16 or wider, within the bound.
No kernel may reach another device: no remote copies, remote signals or barrier semaphores. Data moves between devices by JAX's collectives and lax.ppermute only.
A program may use at most 64 MiB of HBM per device.

v0:
```python
import functools

import jax
import jax.numpy as jnp
from jax import lax
from jax.experimental import pallas as pl
from jax.experimental.pallas import tpu as pltpu
from jax.sharding import PartitionSpec as P

SPAN = 2
TOGETHER = 4
VMEM_LIMIT = 12 * 2**20
F32 = jnp.float32
BF16 = jnp.bfloat16


def dot(a, b):
    return jnp.dot(a, b, preferred_element_type=F32)


def in_vmem(x):
    return pltpu.with_memory_space_constraint(x, pltpu.VMEM)


def in_hbm(x):
    return pltpu.with_memory_space_constraint(x, pltpu.HBM)


def call(kernel, out_shape, vmem_args, smem_args=(), scratch=(), aliases=None, flops=0, fetch=False):
    specs = [pl.BlockSpec(memory_space=pltpu.SMEM)] * len(smem_args)
    for arg in vmem_args:
        if fetch:
            specs.append(pl.BlockSpec(arg.shape, lambda i, n=arg.ndim: (0,) * n))
        else:
            specs.append(pl.BlockSpec(memory_space=pltpu.VMEM))
    return pl.pallas_call(
        kernel,
        grid=(1,) if fetch else (),
        out_shape=out_shape,
        in_specs=specs,
        out_specs=jax.tree.map(lambda _: pl.BlockSpec(memory_space=pltpu.VMEM), out_shape),
        scratch_shapes=list(scratch),
        input_output_aliases=aliases or {},
        compiler_params=pltpu.CompilerParams(vmem_limit_bytes=VMEM_LIMIT),
        cost_estimate=pl.CostEstimate(flops=flops, bytes_accessed=1 << 20, transcendentals=0),
    )(*smem_args, *vmem_args)


def shape(dims, dtype):
    return jax.ShapeDtypeStruct(dims, dtype)


def swap_cores(value):
    n = lax.axis_size("blk")
    return lax.ppermute(value, "blk", [(i, i ^ 1) for i in range(n)])


def paired(value, wanted, by):
    chips = lax.axis_size("blk") // 2
    pairs = []
    for c in range(chips - by):
        if wanted(c):
            for core in range(2):
                low, high = 2 * c + core, 2 * (c + by) + core
                pairs += [(low, high), (high, low)]
    return lax.ppermute(value, "blk", pairs)


def window(value, after=None):
    direct = [
        value,
        paired(value, lambda c: c % 2 == 0, 1),
        paired(value, lambda c: c % 4 < 2, 2),
        paired(value, lambda c: c % 2 == 1, 1),
        paired(value, lambda c: c % 4 >= 2, 2),
    ]
    if after is not None:
        direct[-1], after = lax.optimization_barrier((direct[-1], after))
    return direct + [swap_cores(v) for v in direct], after


def index_kernel(device_ref, cols_ref, delay_ref, slot_ref, *refs):
    count = (len(refs) - 4) // 2
    code_ref, off_ref, list_ref = refs[count : count + 3]
    sems = refs[-1]
    copies = [pltpu.make_async_copy(refs[i], refs[count + 3 + i], sems.at[i]) for i in range(count)]
    for copy in copies:
        copy.start()
    blocks, near = cols_ref.shape
    chip, core = device_ref[0] // 2, device_ref[0] % 2
    base = (chip - SPAN) * 2 * blocks
    top = (2 * SPAN + 1) * 2 * blocks - 1

    def row(b, spot):
        def one(j, spot):
            at = b * near + j
            local = jnp.clip(slot_ref[0, cols_ref[b, j]] - base, 0, top)
            delay = delay_ref[b, j]
            code_ref[at] = local * 8 + delay
            list_ref[spot] = at * 128 + local
            return spot + jnp.where(delay == 1, 1, 0)

        spot = lax.fori_loop(0, near, one, spot, unroll=8)
        list_ref[spot] = b * near * 128 + top + 1
        return spot + spot % 2

    spot = lax.fori_loop(0, blocks, row, 0)
    for i in range(2 * TOGETHER):
        list_ref[spot + i] = top + 1
    list_ref[list_ref.shape[0] - 1] = (spot + 2 * TOGETHER - 1) // (2 * TOGETHER)
    odd = jnp.where(chip % 2 == 0, 1, -1)
    two = jnp.where(chip % 4 < 2, 2, -2)
    for i, rel in enumerate((0, odd, two, -odd, -two)):
        off_ref[i] = ((rel + SPAN) * 2 + core) * blocks
        off_ref[i + 5] = ((rel + SPAN) * 2 + 1 - core) * blocks
    for copy in copies:
        copy.wait()


def start_kernel(past_ref, fin_ref, sinv_ref, fout_ref, coup_ref, pair_ref, delay_ref, pay_ref, mom_ref, send_ref):
    depth, blocks, pulses, _ = past_ref.shape
    rank = fin_ref.shape[1]
    farp = coup_ref.shape[0]
    for p in range(8):
        if p < farp:
            slab = coup_ref[p].astype(BF16)
        elif p == 7:
            row = lax.broadcasted_iota(jnp.int32, (rank, rank), 0)
            rest = jnp.zeros((1, rank - farp), jnp.int32)
            pair, delay = (jnp.concatenate([ref[...], rest], axis=1) for ref in (pair_ref, delay_ref))
            ints = jnp.where(row == 0, pair, jnp.where(row == 1, delay, 0))
            slab = ints.astype(F32).astype(BF16)
        else:
            slab = jnp.zeros((rank, rank), BF16)
        at, side = (p % 4) * rank, (p // 4) * rank
        send_ref[at : at + rank, side : side + rank] = slab
    total = jnp.zeros(mom_ref.shape, F32)
    for b in range(blocks):
        response = dot(fin_ref[b], sinv_ref[b]).astype(BF16)
        rows = [past_ref[0, b], response] + [past_ref[k, b] for k in range(1, depth)]
        whole = jnp.concatenate(rows, axis=0)
        pay_ref[b] = whole
        total = total + dot(whole, fout_ref[b])
    mom_ref[...] = total


def near_sum(step, b, rows, code_ref, tiles_ref, hist_ref, early=False):
    near = tiles_ref.shape[1]
    per_time = hist_ref.shape[0] // 4

    def source(at):
        code = code_ref[at]
        delay, local = code & 7, code >> 3
        if early:
            local = jnp.where(delay == 1, per_time - 1, local)
        return hist_ref[((step - delay) & 3) * per_time + local, :rows, :]

    acc = jnp.zeros((rows, tiles_ref.shape[3]), F32)
    for j in range(0, near, 2):
        at = b * near + j
        both = jnp.concatenate([source(at), source(at + 1)], axis=1)
        tile = tiles_ref[b, j : j + 2].reshape(-1, tiles_ref.shape[3])
        acc = acc + dot(both, tile)
    return acc


def early_kernel(step, code_ref, tiles_ref, hist_ref, acc_ref):
    def row(b, _):
        acc_ref[b] = near_sum(step, b, acc_ref.shape[1], code_ref, tiles_ref, hist_ref, early=True)
        return 0

    lax.fori_loop(0, acc_ref.shape[0], row, 0)


def step_kernel(step, last, packs, *refs):
    refs = list(refs)
    code_ref, off_ref, list_ref = refs[:3]
    pieces = refs[3:13]
    tiles_ref, inc_ref, sinv_ref, fout_ref = refs[13:17]
    rest = refs[17:]
    moms = []
    if step > 0:
        early_ref, sum_ref = rest[1], rest[-1]
        rest = rest[2:-1]
    if packs:
        moms, rest = rest[:packs], rest[packs:]
    blocks, near = tiles_ref.shape[:2]
    pulses = inc_ref.shape[2]
    if last:
        loc_ref, hist_ref = rest
        rows = pulses
    else:
        hist_ref, pay_ref, mom_ref = rest[:3]
        rows = pay_ref.shape[1]
    per_time = hist_ref.shape[0] // 4
    held = hist_ref.shape[1]

    if step == 0:
        for k in range(1, 4):
            hist_ref[pl.ds((3 - k) * per_time, per_time), pulses:held, :] = jnp.zeros(
                (per_time, held - pulses, hist_ref.shape[2]), BF16
            )
        for k in range(4):
            hist_ref[(k + 1) * per_time - 1] = jnp.zeros(hist_ref.shape[1:], BF16)
    for i, piece in enumerate(pieces):
        off = off_ref[i]
        if step == 0:
            hist_ref[pl.ds(3 * per_time + off, blocks), :, :] = piece[:, :held, :]
            for k in range(1, 4):
                row = held + (k - 1) * pulses
                hist_ref[pl.ds((3 - k) * per_time + off, blocks), :pulses, :] = piece[:, row : row + pulses, :]
        else:
            hist_ref[pl.ds(((step - 1) % 4) * per_time + off, blocks), :rows, :] = piece[...]

    if step > 0:
        newest = ((step - 1) & 3) * per_time
        sum_ref[...] = early_ref[...]

        def turn(i, _):
            sums = []
            for pair in range(TOGETHER):
                one, two = (list_ref[(i * TOGETHER + pair) * 2 + k] for k in range(2))
                both = jnp.concatenate([hist_ref[newest + (c & 127), :rows, :] for c in (one, two)], axis=1)
                at = [c >> 7 for c in (one, two)]
                tile = jnp.concatenate([tiles_ref[t // near, t % near] for t in at], axis=0)
                sums.append((at[0] // near, dot(both, tile)))
            for b, value in sums:
                sum_ref[b] += value
            return 0

        lax.fori_loop(0, list_ref[list_ref.shape[0] - 1], turn, 0)

    def row(b, total):
        if step == 0:
            acc = near_sum(step, b, rows, code_ref, tiles_ref, hist_ref)
        else:
            acc = sum_ref[b]
        main = inc_ref[step, b].astype(F32) - acc[:pulses]
        driven = main if last else jnp.concatenate([main, -acc[pulses:]], axis=0)
        current = dot(driven.astype(BF16), sinv_ref[b])
        if last:
            loc_ref[b] = current
            return total
        rounded = current.astype(BF16)
        pay_ref[b] = rounded
        return total + dot(rounded, fout_ref[b])

    start = jnp.zeros((rows, fout_ref.shape[2]), F32)
    total = lax.fori_loop(0, blocks, row, start, unroll=step > 0)
    if last:
        return
    if not packs:
        mom_ref[...] = total
        return
    main_ref = rest[3]
    main_ref[...] = pay_ref[:, :pulses, :]
    listed = [m[...] for m in moms] + [total[:pulses]]
    every = jnp.concatenate(listed, axis=0).astype(BF16)
    half, rank = every.shape[0] // 2, every.shape[1]
    mom_ref[:half, :rank] = every[:half]
    mom_ref[:half, rank:] = every[half:]
    mom_ref[half:, :] = jnp.zeros((mom_ref.shape[0] - half, mom_ref.shape[1]), BF16)


def sum_kernel(in_ref, out_ref):
    total = in_ref[0].astype(F32)
    for i in range(1, in_ref.shape[0]):
        total = total + in_ref[i].astype(F32)
    for i in range(out_ref.shape[0]):
        out_ref[i] = total.astype(BF16)


def halves_kernel(place_ref, sums_ref, coup_ref, out_ref):
    core = place_ref[1]
    for i, ref in ((0, sums_ref), (sums_ref.shape[0] // 2, coup_ref)):
        rows = ref.shape[0] // 2
        half = ref[pl.ds(pl.multiple_of(core * rows, rows), rows), :]
        for g in range(out_ref.shape[0]):
            out_ref[g, i : i + rows, :] = half


def finish_kernel(steps, farp, place_ref, mine_ref, other_ref, *refs):
    pays = refs[:steps]
    loc_ref, out_ref, got_ref, coup_ref, low_ref, high_ref, qrev_ref, c_ref, bl_ref, a_ref, ints_ref, num_ref, sem = refs[steps:]
    regions = got_ref.shape[0]
    depth = 4
    blocks, pulses = loc_ref.shape[:2]
    rank = coup_ref.shape[2] // 2
    held = pulses + rank
    first = held + (depth - 1) * pulses
    half = (first + (steps - 2) * held + pulses) // 2

    for ref, core in ((mine_ref, place_ref[1]), (other_ref, 1 - place_ref[1])):
        for whole, at in ((got_ref, 0), (coup_ref, got_ref.shape[1] // 2)):
            rows = whole.shape[1] // 2
            whole[:, pl.ds(pl.multiple_of(core * rows, rows), rows), :] = ref[:, at : at + rows, :]

    ints_ref[...] = jnp.zeros(ints_ref.shape, jnp.int32)
    for g in range(regions):
        numbers = coup_ref[g, 3 * rank : 3 * rank + 16, rank:].astype(F32).astype(jnp.int32)
        ints_ref[2 * g : 2 * g + 2, :rank] = numbers[:2]
    copy = pltpu.make_async_copy(ints_ref, num_ref, sem)
    copy.start()

    def rows_of(g, at, count):
        parts = []
        for r in range(at, at + count, 16):
            side, row = divmod(r, half)
            parts.append(got_ref[g, row : row + 16, side * rank : (side + 1) * rank])
        return jnp.concatenate(parts, axis=0)

    def keep(time, g, value):
        low_ref[(time + depth) * regions + g, :, :rank] = value
        high_ref[(time + depth) * regions + g, :, rank:] = value

    def source(n, g, q):
        return (n - num_ref[2 * g + 1, q] + depth) * regions + num_ref[2 * g, q]

    low_ref[...] = jnp.zeros(low_ref.shape, BF16)
    high_ref[...] = jnp.zeros(high_ref.shape, BF16)
    bl_ref[...] = jnp.zeros(bl_ref.shape, BF16)
    a_ref[...] = jnp.zeros(a_ref.shape, BF16)
    for g in range(regions):
        keep(-1, g, rows_of(g, 0, pulses))
        for k in range(1, depth):
            keep(-1 - k, g, rows_of(g, held + (k - 1) * pulses, pulses))
        for lag in range(steps - 1):
            at = pulses if lag == 0 else first + (lag - 1) * held + pulses
            spot = (steps - 2 - lag) * rank
            qrev_ref[g, spot : spot + rank, :] = rows_of(g, at, rank)
        qrev_ref[g, (steps - 1) * rank :, :] = jnp.zeros((rank, rank), BF16)
        for p in range(8):
            c_ref[g, p * rank : (p + 1) * rank, :] = (
                coup_ref[g, (p % 4) * rank : (p % 4 + 1) * rank, (p // 4) * rank : (p // 4 + 1) * rank]
                if p < farp
                else jnp.zeros((rank, rank), BF16)
            )

    copy.wait()
    for n in range(steps):
        blended = []
        for g in range(regions):
            acc = jnp.zeros((pulses, rank), F32)
            for p in range(0, farp, 4):
                lanes = []
                for q in range(p, min(p + 4, farp), 2):
                    part = low_ref[source(n, g, q)]
                    if q + 1 < farp:
                        part = part + high_ref[source(n, g, q + 1)]
                    lanes.append(part)
                lhs = jnp.concatenate(lanes, axis=1)
                acc = acc + dot(lhs, c_ref[g, p * rank : p * rank + lhs.shape[1], :])
            blended.append(acc.astype(BF16))
        for g in range(regions):
            bl_ref[g, :, n * rank : (n + 1) * rank] = blended[g]
        if n < steps - 1:
            depth_k = 2 * rank * ((n + 2) // 2)
            at = first + n * held
            spot = (steps - 2 - n) * rank
            for g in range(regions):
                change = dot(bl_ref[g, :, :depth_k], qrev_ref[g, spot : spot + depth_k, :])
                keep(n, g, (rows_of(g, at, pulses).astype(F32) - change).astype(BF16))

    mine = place_ref[0]
    for n in range(steps):
        a_ref[n * pulses : (n + 1) * pulses, (steps - 1 - n) * rank :] = bl_ref[mine, :, : (n + 1) * rank]
    for b in range(blocks):
        response = jnp.concatenate([pays[k][b, pulses : pulses + rank, :] for k in reversed(range(steps))], axis=0)
        far = dot(a_ref[...], response)
        for n in range(steps):
            local = loc_ref[b] if n == steps - 1 else pays[n + 1][b, :pulses, :].astype(F32)
            out_ref[n, b] = (local - far[n * pulses : (n + 1) * pulses]).astype(BF16)


def on_device(
    incident,
    past_currents,
    self_inverse,
    near_tiles,
    near_cols,
    near_delay,
    block_slot,
    far_out,
    far_in,
    far_pairs,
    far_delay,
    far_coupling,
):
    steps, _, blocks, pulses, rows = incident.shape
    depth = past_currents.shape[0]
    near = near_cols.shape[2]
    farp, rank = far_coupling.shape[1:3]
    regions = lax.axis_size("region")
    ring = lax.axis_size("blk")
    device = lax.axis_index("blk")
    held = pulses + rank
    near_blocks = (2 * SPAN + 1) * 2 * blocks + 1

    past, fin = past_currents[:, 0], far_in[0]

    first = held + (depth - 1) * pulses
    payload, moment, coupling = call(
        start_kernel,
        (
            shape((blocks, first, rows), BF16),
            shape((first, rank), F32),
            shape((4 * rank, 2 * rank), BF16),
        ),
        [in_hbm(x) for x in (past, fin, self_inverse[0], far_out[0], far_coupling[0], far_pairs, far_delay)],
        fetch=True,
    )
    fetched = [near_tiles[0], incident[:, 0], self_inverse[0], far_out[0]]
    code, offsets, late, tiles, inc, sinv, fout = pl.pallas_call(
        index_kernel,
        out_shape=(
            shape((blocks * near,), jnp.int32),
            shape((10,), jnp.int32),
            shape((blocks * (near + 1) + 2 * TOGETHER + 8,), jnp.int32),
            *(shape(x.shape, x.dtype) for x in fetched),
        ),
        in_specs=[pl.BlockSpec(memory_space=pltpu.SMEM)] * 4 + [pl.BlockSpec(memory_space=pltpu.HBM)] * 4,
        out_specs=(pl.BlockSpec(memory_space=pltpu.SMEM),) * 3 + (pl.BlockSpec(memory_space=pltpu.VMEM),) * 4,
        scratch_shapes=[pltpu.SemaphoreType.DMA((4,))],
        compiler_params=pltpu.CompilerParams(vmem_limit_bytes=VMEM_LIMIT),
        cost_estimate=pl.CostEstimate(flops=0, bytes_accessed=1 << 24, transcendentals=0),
    )(
        device.astype(jnp.int32).reshape(1),
        near_cols[0],
        near_delay[0],
        block_slot,
        *(in_hbm(x) for x in fetched),
    )
    pays, moms = [payload], [moment]
    hist = None
    hist_shape = shape((4 * near_blocks, held, rows), BF16)
    flops = 2 * blocks * near * held * rows * rows
    for n in range(steps):
        last = n == steps - 1
        packs = len(moms) if n == steps - 2 else 0
        tail, aliases, scratch = [], {}, []
        if n == 0:
            pieces, code = window(payload, code)
        else:
            wide = pulses if last else held
            early = call(
                functools.partial(early_kernel, n),
                shape((blocks, wide, rows), F32),
                [in_vmem(tiles), in_vmem(hist)],
                [code],
                flops=flops,
            )
            pieces, early = window(payload, early)
            tail = [in_vmem(hist), early]
            scratch = [pltpu.VMEM((blocks, wide, rows), F32)]
        args = pieces + [in_vmem(tiles), inc, sinv, fout] + tail
        if n > 0:
            aliases = {3 + len(args) - 2: 1 if last else 0}
        loc_shape = shape((blocks, pulses, rows), F32)
        if last:
            outs = (loc_shape, hist_shape)
        elif packs:
            args += moms
            outs = (
                hist_shape,
                shape((blocks, held, rows), BF16),
                shape((512, 2 * rank), BF16),
                shape((blocks, pulses, rows), BF16),
            )
        else:
            outs = (hist_shape, shape((blocks, held, rows), BF16), shape((held, rank), F32))
        got = call(
            functools.partial(step_kernel, n, last, packs),
            outs,
            args,
            [code, offsets, late],
            scratch=scratch,
            aliases=aliases,
            flops=flops,
        )
        if last:
            loc = got[0]
        elif packs:
            hist, payload, packed, main = got
            pays.append(payload)
            payload = main
        else:
            hist, payload, moment = got
            pays.append(payload)
            moms.append(moment)

    packed, loc = lax.optimization_barrier((packed, loc))
    shares = lax.all_to_all(packed.reshape(ring, 512 // ring, 2 * rank), "blk", 0, 0, tiled=True)
    sums = call(sum_kernel, shape(shares.shape, BF16), [shares])
    sums = lax.all_to_all(sums, "blk", 0, 0, tiled=True).reshape(512, 2 * rank)
    place = jnp.stack([lax.axis_index("region"), device % 2]).astype(jnp.int32)
    halves = call(halves_kernel, shape((regions, 256 + 2 * rank, 2 * rank), BF16), [sums, coupling], [place])
    halves = lax.all_to_all(halves, "region", 0, 0, tiled=True)
    others = swap_cores(halves)

    currents = call(
        functools.partial(finish_kernel, steps, farp),
        shape((steps, blocks, pulses, rows), BF16),
        [halves, others, *pays, loc],
        [place],
        scratch=[
            pltpu.VMEM((regions, 512, 2 * rank), BF16),
            pltpu.VMEM((regions, 4 * rank, 2 * rank), BF16),
            pltpu.VMEM(((depth + steps) * regions, pulses, 2 * rank), BF16),
            pltpu.VMEM(((depth + steps) * regions, pulses, 2 * rank), BF16),
            pltpu.VMEM((regions, steps * rank, rank), BF16),
            pltpu.VMEM((regions, 8 * rank, rank), BF16),
            pltpu.VMEM((regions, pulses, steps * rank), BF16),
            pltpu.VMEM((steps * pulses, steps * rank), BF16),
            pltpu.VMEM((2 * regions, 128), jnp.int32),
            pltpu.SMEM((2 * regions, 128), jnp.int32),
            pltpu.SemaphoreType.DMA,
        ],
    )
    return currents[:, None]


def solution(mesh):
    in_specs = (
        P(None, "region", "blk", None, None),
        P(None, "region", "blk", None, None),
        P("region", "blk", None, None),
        P("region", "blk", None, None, None),
        P("region", "blk", None),
        P("region", "blk", None),
        P("region", None),
        P("region", "blk", None, None),
        P("region", "blk", None, None),
        P("region", None),
        P("region", None),
        P("region", None, None, None),
    )
    out_specs = P(None, "region", "blk", None, None)
    return jax.shard_map(on_device, mesh=mesh, in_specs=in_specs, out_specs=out_specs, check_vma=False)
```

profile of v0, /device:TPU:1, one launch (start us, length us, event | category | flops | bytes accessed | tf_op | source)
XLA Modules:
  0.0 302.6 jit_solution(12832807489626239330)
XLA Ops:
  5.0 10.6 %collective-permute-start.2 = (bf16[8,192,128]{2,1,0:T(8,128)(2,1)S(1)}, bf16[8,192,128]{2,1,0:T(8,128)(2,1)S(1)}, u32[]{:S(2)}, u32[]{:S(2)}) collective-permute-start(bf16[8,192,128]{2,1,0:T(8,128)(2,1)S(1)} %get-tuple-element.56.refs_3_.refs_0_), channel_id=1, source_target_pairs={{0,4},{4,0},{1,5},{5,1},{2,6},{6,2},{3,7},{7,3},{8,12},{12,8},{9,1... | collective-permute-start | bytes 1179656 | tf_op jit(solution)/shard_map/ppermute | solution.py:66
  19.8 4.9 %shard_map.119 = (s32[256]{0:T(256)S(1)}, s32[10]{0:T(128)S(1)}, s32[280]{0:T(512)S(1)}, bf16[8,32,128,128]{3,2,1,0:T(8,128)(2,1)S(1)}, bf16[8,8,32,128]{3,2,1,0...) custom-call(s32[1]{0:T(128)} %bitcast.7.device_ref, s32[8,32]{1,0:T(8,128)S(1)} %bitcast.19, ...), custom_call_target="tpu_custom_call" | custom-call | bytes 16777216 | tf_op jit(solution)/shard_map/pallas_call | solution.py:413
  24.9 15.9 %collective-permute-done.2.refs_5_ = bf16[8,192,128]{2,1,0:T(8,128)(2,1)S(1)} collective-permute-done((bf16[8,192,128]{2,1,0:T(8,128)(2,1)S(1)}, bf16[8,192,128]{2,1,0:T(8,128)(2,1)S(1)}, u32[]{:S(2)}, u32[]{:S(2)}) %collective-permute-start.2) | collective-permute-done | bytes 393248 | tf_op jit(solution)/shard_map/ppermute | solution.py:66
  44.8 6.3 %shard_map.120 = (bf16[324,96,128]{2,1,0:T(8,128)(2,1)S(1)}, bf16[8,96,128]{2,1,0:T(8,128)(2,1)S(1)}, f32[96,64]{1,0:T(8,128)S(1)}) custom-call(s32[256]{0:T(256)S(1)} %get-tuple-element.58.refs_0_.code_ref, s32[10]{0:T(128)S(1)} %get-tuple-element.59.refs_1_, s32[280]{0:T(512)S(1)} %get-tuple-element.60.refs_2_, ...), custom_call_target="tpu_custom_call" | custom-call | flops 805306368 | bytes 1048576 | tf_op jit(solution)/shard_map/pallas_call | solution.py:36
  52.4 4.7 %collective-permute-start.10 = (bf16[8,96,128]{2,1,0:T(8,128)(2,1)S(1)}, bf16[8,96,128]{2,1,0:T(8,128)(2,1)S(1)}, u32[]{:S(2)}, u32[]{:S(2)}) collective-permute-start(bf16[8,96,128]{2,1,0:T(8,128)(2,1)S(1)} %get-tuple-element.66.refs_3_.refs_1_), channel_id=1, source_target_pairs={{0,4},{4,0},{1,5},{5,1},{2,6},{6,2},{3,7},{7,3},{8,12},{12,8},{9,1... | collective-permute-start | bytes 589832 | tf_op jit(solution)/shard_map/ppermute | solution.py:66
  61.8 3.6 %shard_map.121.refs_18_ = f32[8,96,128]{2,1,0:T(8,128)S(1)} custom-call(s32[256]{0:T(256)S(1)} %get-tuple-element.58.refs_0_.code_ref, bf16[8,32,128,128]{3,2,1,0:T(8,128)(2,1)S(1)} %get-tuple-element.62.refs_13_.tiles_ref, bf16[324,96,128]{2,1,0:T(8,128)(2,1)S(1)} %get-tuple-element.67.hist_ref.refs_17_), custom_call_target="tpu_custom_call" | custom-call | flops 805306368 | bytes 1048576 | tf_op jit(solution)/shard_map/pallas_call | solution.py:36
  65.6 4.6 %collective-permute-done.10.refs_5_ = bf16[8,96,128]{2,1,0:T(8,128)(2,1)S(1)} collective-permute-done((bf16[8,96,128]{2,1,0:T(8,128)(2,1)S(1)}, bf16[8,96,128]{2,1,0:T(8,128)(2,1)S(1)}, u32[]{:S(2)}, u32[]{:S(2)}) %collective-permute-start.10) | collective-permute-done | bytes 196640 | tf_op jit(solution)/shard_map/ppermute | solution.py:66
  77.8 7.7 %collective-permute-start.19 = (bf16[8,96,128]{2,1,0:T(8,128)(2,1)S(1)}, bf16[8,96,128]{2,1,0:T(8,128)(2,1)S(1)}, u32[]{:S(2)}, u32[]{:S(2)}) collective-permute-start(bf16[8,96,128]{2,1,0:T(8,128)(2,1)S(1)} %get-tuple-element.70.refs_3_.refs_2_), channel_id=1, source_target_pairs={{0,4},{4,0},{1,5},{5,1},{2,6},{6,2},{3,7},{7,3},{8,12},{12,8},{9,1... | collective-permute-start | bytes 589832 | tf_op jit(solution)/shard_map/ppermute | solution.py:66
  88.2 3.6 %shard_map.123.refs_18_ = f32[8,96,128]{2,1,0:T(8,128)S(1)} custom-call(s32[256]{0:T(256)S(1)} %get-tuple-element.58.refs_0_.code_ref, bf16[8,32,128,128]{3,2,1,0:T(8,128)(2,1)S(1)} %get-tuple-element.62.refs_13_.tiles_ref, bf16[324,96,128]{2,1,0:T(8,128)(2,1)S(1)} %get-tuple-element.71.hist_ref.refs_17_), custom_call_target="tpu_custom_call" | custom-call | flops 805306368 | bytes 1048576 | tf_op jit(solution)/shard_map/pallas_call | solution.py:36
  91.9 6.7 %collective-permute-done.19.refs_5_ = bf16[8,96,128]{2,1,0:T(8,128)(2,1)S(1)} collective-permute-done((bf16[8,96,128]{2,1,0:T(8,128)(2,1)S(1)}, bf16[8,96,128]{2,1,0:T(8,128)(2,1)S(1)}, u32[]{:S(2)}, u32[]{:S(2)}) %collective-permute-start.19) | collective-permute-done | bytes 196640 | tf_op jit(solution)/shard_map/ppermute | solution.py:66
  106.2 5.3 %collective-permute-start.28 = (bf16[8,96,128]{2,1,0:T(8,128)(2,1)S(1)}, bf16[8,96,128]{2,1,0:T(8,128)(2,1)S(1)}, u32[]{:S(2)}, u32[]{:S(2)}) collective-permute-start(bf16[8,96,128]{2,1,0:T(8,128)(2,1)S(1)} %get-tuple-element.74.refs_3_), channel_id=1, source_target_pairs={{0,4},{4,0},{1,5},{5,1},{2,6},{6,2},{3,7},{7,3},{8,12},{12,8},{9,1... | collective-permute-start | bytes 589832 | tf_op jit(solution)/shard_map/ppermute | solution.py:66
  115.7 3.6 %shard_map.125.refs_18_ = f32[8,96,128]{2,1,0:T(8,128)S(1)} custom-call(s32[256]{0:T(256)S(1)} %get-tuple-element.58.refs_0_.code_ref, bf16[8,32,128,128]{3,2,1,0:T(8,128)(2,1)S(1)} %get-tuple-element.62.refs_13_.tiles_ref, bf16[324,96,128]{2,1,0:T(8,128)(2,1)S(1)} %get-tuple-element.75.hist_ref.refs_17_), custom_call_target="tpu_custom_call" | custom-call | flops 805306368 | bytes 1048576 | tf_op jit(solution)/shard_map/pallas_call | solution.py:36
  119.4 5.2 %collective-permute-done.28.refs_5_ = bf16[8,96,128]{2,1,0:T(8,128)(2,1)S(1)} collective-permute-done((bf16[8,96,128]{2,1,0:T(8,128)(2,1)S(1)}, bf16[8,96,128]{2,1,0:T(8,128)(2,1)S(1)}, u32[]{:S(2)}, u32[]{:S(2)}) %collective-permute-start.28) | collective-permute-done | bytes 196640 | tf_op jit(solution)/shard_map/ppermute | solution.py:66
  132.2 7.2 %collective-permute-start.37 = (bf16[8,96,128]{2,1,0:T(8,128)(2,1)S(1)}, bf16[8,96,128]{2,1,0:T(8,128)(2,1)S(1)}, u32[]{:S(2)}, u32[]{:S(2)}) collective-permute-start(bf16[8,96,128]{2,1,0:T(8,128)(2,1)S(1)} %get-tuple-element.78.refs_3_.refs_4_), channel_id=1, source_target_pairs={{0,4},{4,0},{1,5},{5,1},{2,6},{6,2},{3,7},{7,3},{8,12},{12,8},{9,1... | collective-permute-start | bytes 589832 | tf_op jit(solution)/shard_map/ppermute | solution.py:66
  142.2 3.7 %shard_map.127.refs_18_ = f32[8,96,128]{2,1,0:T(8,128)S(1)} custom-call(s32[256]{0:T(256)S(1)} %get-tuple-element.58.refs_0_.code_ref, bf16[8,32,128,128]{3,2,1,0:T(8,128)(2,1)S(1)} %get-tuple-element.62.refs_13_.tiles_ref, bf16[324,96,128]{2,1,0:T(8,128)(2,1)S(1)} %get-tuple-element.79.hist_ref.refs_17_), custom_call_target="tpu_custom_call" | custom-call | flops 805306368 | bytes 1048576 | tf_op jit(solution)/shard_map/pallas_call | solution.py:36
  146.0 6.4 %collective-permute-done.37.refs_5_ = bf16[8,96,128]{2,1,0:T(8,128)(2,1)S(1)} collective-permute-done((bf16[8,96,128]{2,1,0:T(8,128)(2,1)S(1)}, bf16[8,96,128]{2,1,0:T(8,128)(2,1)S(1)}, u32[]{:S(2)}, u32[]{:S(2)}) %collective-permute-start.37) | collective-permute-done | bytes 196640 | tf_op jit(solution)/shard_map/ppermute | solution.py:66
  153.6 8.6 %collective-permute-start.41 = (bf16[8,96,128]{2,1,0:T(8,128)(2,1)S(1)}, bf16[8,96,128]{2,1,0:T(8,128)(2,1)S(1)}, u32[]{:S(2)}, u32[]{:S(2)}) collective-permute-start(bf16[8,96,128]{2,1,0:T(8,128)(2,1)S(1)} %collective-permute-done.36.refs_4_), channel_id=1, source_target_pairs={{0,1},{1,0},{2,3},{3,2},{4,5},{5,4},{6,7},{7,6},{8,9},{9,8},{10,11... | collective-permute-start | bytes 589832 | tf_op jit(solution)/shard_map/ppermute | solution.py:55
  163.9 3.4 %shard_map.128 = (bf16[324,96,128]{2,1,0:T(8,128)(2,1)S(1)}, bf16[8,96,128]{2,1,0:T(8,128)(2,1)S(1)}, f32[96,64]{1,0:T(8,128)S(1)}) custom-call(s32[256]{0:T(256)S(1)} %get-tuple-element.58.refs_0_.code_ref, s32[10]{0:T(128)S(1)} %get-tuple-element.59.refs_1_, s32[280]{0:T(512)S(1)} %get-tuple-element.60.refs_2_, ...), custom_call_target="tpu_custom_call", output_to_operand_aliasing={{0}: (17, {})} | custom-call | flops 805306368 | bytes 1048576 | tf_op jit(solution)/shard_map/pallas_call | solution.py:36
  168.7 5.2 %collective-permute-start.46 = (bf16[8,96,128]{2,1,0:T(8,128)(2,1)S(1)}, bf16[8,96,128]{2,1,0:T(8,128)(2,1)S(1)}, u32[]{:S(2)}, u32[]{:S(2)}) collective-permute-start(bf16[8,96,128]{2,1,0:T(8,128)(2,1)S(1)} %get-tuple-element.82.refs_3_.refs_5_), channel_id=1, source_target_pairs={{0,4},{4,0},{1,5},{5,1},{2,6},{6,2},{3,7},{7,3},{8,12},{12,8},{9,1... | collective-permute-start | bytes 589832 | tf_op jit(solution)/shard_map/ppermute | solution.py:66
  173.9 3.8 %collective-permute-start.45 = (bf16[8,96,128]{2,1,0:T(8,128)(2,1)S(1)}, bf16[8,96,128]{2,1,0:T(8,128)(2,1)S(1)}, u32[]{:S(2)}, u32[]{:S(2)}) collective-permute-start(bf16[8,96,128]{2,1,0:T(8,128)(2,1)S(1)} %get-tuple-element.82.refs_3_.refs_5_), channel_id=1, source_target_pairs={{0,2},{2,0},{1,3},{3,1},{4,6},{6,4},{5,7},{7,5},{8,10},{10,8},{9,1... | collective-permute-start | bytes 589832 | tf_op jit(solution)/shard_map/ppermute | solution.py:66
  178.7 3.6 %shard_map.129.refs_18_ = f32[8,96,128]{2,1,0:T(8,128)S(1)} custom-call(s32[256]{0:T(256)S(1)} %get-tuple-element.58.refs_0_.code_ref, bf16[8,32,128,128]{3,2,1,0:T(8,128)(2,1)S(1)} %get-tuple-element.62.refs_13_.tiles_ref, bf16[324,96,128]{2,1,0:T(8,128)(2,1)S(1)} %get-tuple-element.83.hist_ref.refs_17_), custom_call_target="tpu_custom_call" | custom-call | flops 805306368 | bytes 1048576 | tf_op jit(solution)/shard_map/pallas_call | solution.py:36
  194.6 7.2 %collective-permute-start.55 = (bf16[8,96,128]{2,1,0:T(8,128)(2,1)S(1)}, bf16[8,96,128]{2,1,0:T(8,128)(2,1)S(1)}, u32[]{:S(2)}, u32[]{:S(2)}) collective-permute-start(bf16[8,96,128]{2,1,0:T(8,128)(2,1)S(1)} %get-tuple-element.86.refs_3_.refs_6_), channel_id=1, source_target_pairs={{0,4},{4,0},{1,5},{5,1},{2,6},{6,2},{3,7},{7,3},{8,12},{12,8},{9,1... | collective-permute-start | bytes 589832 | tf_op jit(solution)/shard_map/ppermute | solution.py:66
  205.8 3.6 %shard_map.131.refs_18_ = f32[8,96,128]{2,1,0:T(8,128)S(1)} custom-call(s32[256]{0:T(256)S(1)} %get-tuple-element.58.refs_0_.code_ref, bf16[8,32,128,128]{3,2,1,0:T(8,128)(2,1)S(1)} %get-tuple-element.62.refs_13_.tiles_ref, bf16[324,96,128]{2,1,0:T(8,128)(2,1)S(1)} %get-tuple-element.87.hist_ref.refs_17_), custom_call_target="tpu_custom_call" | custom-call | flops 805306368 | bytes 1048576 | tf_op jit(solution)/shard_map/pallas_call | solution.py:36
  209.6 5.2 %collective-permute-done.55.refs_5_ = bf16[8,96,128]{2,1,0:T(8,128)(2,1)S(1)} collective-permute-done((bf16[8,96,128]{2,1,0:T(8,128)(2,1)S(1)}, bf16[8,96,128]{2,1,0:T(8,128)(2,1)S(1)}, u32[]{:S(2)}, u32[]{:S(2)}) %collective-permute-start.55) | collective-permute-done | bytes 196640 | tf_op jit(solution)/shard_map/ppermute | solution.py:66
  217.7 3.7 %shard_map.132 = (bf16[324,96,128]{2,1,0:T(8,128)(2,1)S(1)}, bf16[8,96,128]{2,1,0:T(8,128)(2,1)S(1)}, bf16[512,128]{1,0:T(8,128)(2,1)S(1)}, bf16[8,32,128]{2,1,0:T(8,128)(2,1)S(1)}) custom-call(s32[256]{0:T(256)S(1)} %get-tuple-element.58.refs_0_.code_ref, s32[10]{0:T(128)S(1)} %get-tuple-element.59.refs_1_, ...), custom_call_target="tpu_custom_call", output_to_operand_aliasing={{0}: (17, {})} | custom-call | flops 805306368 | bytes 1048576 | tf_op jit(solution)/shard_map/pallas_call | solution.py:36
  222.8 6.0 %collective-permute-start.64 = (bf16[8,32,128]{2,1,0:T(8,128)(2,1)S(1)}, bf16[8,32,128]{2,1,0:T(8,128)(2,1)S(1)}, u32[]{:S(2)}, u32[]{:S(2)}) collective-permute-start(bf16[8,32,128]{2,1,0:T(8,128)(2,1)S(1)} %get-tuple-element.98.refs_3_), channel_id=1, source_target_pairs={{0,4},{4,0},{1,5},{5,1},{2,6},{6,2},{3,7},{7,3},{8,12},{12,8},{9,1... | collective-permute-start | bytes 196616 | tf_op jit(solution)/shard_map/ppermute | solution.py:66
  228.8 3.7 %collective-permute-start.63 = (bf16[8,32,128]{2,1,0:T(8,128)(2,1)S(1)}, bf16[8,32,128]{2,1,0:T(8,128)(2,1)S(1)}, u32[]{:S(2)}, u32[]{:S(2)}) collective-permute-start(bf16[8,32,128]{2,1,0:T(8,128)(2,1)S(1)} %get-tuple-element.98.refs_3_), channel_id=1, source_target_pairs={{0,2},{2,0},{1,3},{3,1},{4,6},{6,4},{5,7},{7,5},{8,10},{10,8},{9,1... | collective-permute-start | bytes 196616 | tf_op jit(solution)/shard_map/ppermute | solution.py:66
  241.5 12.6 %all_to_all.15.in_ref = bf16[32,16,128]{2,1,0:T(8,128)(2,1)S(1)} all-to-all(bf16[32,16,128]{2,1,0:T(8,128)(2,1)S(1)} %bitcast.18), channel_id=1, replica_groups=mesh['region'=8,'blk'=32] {'blk'}, dimensions={0} | all-to-all | bytes 262144 | tf_op jit(solution)/shard_map/all_to_all | solution.py:492
  254.8 5.1 %all-to-all-start.1 = ((bf16[32,16,128]{2,1,0:T(8,128)(2,1)}), bf16[32,16,128]{2,1,0:T(8,128)(2,1)S(1)}, u32[]{:S(2)}, u32[]{:S(2)}) async-start(bf16[32,16,128]{2,1,0:T(8,128)(2,1)} %shard_map.135), calls=%async_computation.1 | async-start | bytes 262144 | tf_op jit(solution)/shard_map/all_to_all | solution.py:494
  260.0 9.1 %all-to-all-done.1 = bf16[32,16,128]{2,1,0:T(8,128)(2,1)S(1)} async-done(((bf16[32,16,128]{2,1,0:T(8,128)(2,1)}), bf16[32,16,128]{2,1,0:T(8,128)(2,1)S(1)}, u32[]{:S(2)}, u32[]{:S(2)}) %all-to-all-start.1) | async-done | bytes 131104 | tf_op jit(solution)/shard_map/all_to_all | solution.py:494
  269.7 20.1 %all_to_all.16.mine_ref = bf16[8,384,128]{2,1,0:T(8,128)(2,1)S(1)} all-to-all(bf16[8,384,128]{2,1,0:T(8,128)(2,1)S(1)} %shard_map.136), channel_id=1, replica_groups=mesh['region'=8,'blk'=32] {'region'}, dimensions={0} | all-to-all | bytes 1572864 | tf_op jit(solution)/shard_map/all_to_all | solution.py:497
  294.9 7.4 %shard_map.137 = bf16[8,8,32,128]{3,2,1,0:T(8,128)(2,1)} custom-call(s32[2]{0:T(128)S(1)} %pad_add_fusion.place_ref, bf16[8,384,128]{2,1,0:T(8,128)(2,1)S(1)} %all_to_all.16.mine_ref, bf16[8,384,128]{2,1,0:T(8,128)(2,1)S(1)} %collective-permute-done.72.other_ref, bf16[8,192,128]{2,1,0:T(8,128)(2,1)S(1)} %get-tuple-element.56.refs_3_.refs_0_, ...), custom_call_target="tpu_custom_call" | custom-call | bytes 1048576 | tf_op jit(solution)/shard_map/pallas_call | solution.py:36
  (146 shorter events, 93.4 us)
Async XLA Ops:
  3.6 21.2 %collective-permute-start = (bf16[8,192,128]{2,1,0:T(8,128)(2,1)S(1)}, bf16[8,192,128]{2,1,0:T(8,128)(2,1)S(1)}, u32[]{:S(2)}, u32[]{:S(2)}) collective-permute-start(bf16[8,192,128]{2,1,0:T(8,128)(2,1)S(1)} %get-tuple-element.56.refs_3_.refs_0_), channel_id=1, source_target_pairs={{4,8},{8,4},{5,9},{9,5},{6,10},{10,6},{7,11},{11,7},{12,16},{16,12... | collective-permute-start | bytes 1179656 | tf_op jit(solution)/shard_map/ppermute | solution.py:66
  4.3 20.5 %collective-permute-start.3 = (bf16[8,192,128]{2,1,0:T(8,128)(2,1)S(1)}, bf16[8,192,128]{2,1,0:T(8,128)(2,1)S(1)}, u32[]{:S(2)}, u32[]{:S(2)}) collective-permute-start(bf16[8,192,128]{2,1,0:T(8,128)(2,1)S(1)} %get-tuple-element.56.refs_3_.refs_0_), channel_id=1, source_target_pairs={{2,4},{4,2},{3,5},{5,3},{6,8},{8,6},{7,9},{9,7},{10,12},{12,10},{1... | collective-permute-start | bytes 1179656 | tf_op jit(solution)/shard_map/ppermute | solution.py:66
  5.0 35.8 %collective-permute-start.2 = (bf16[8,192,128]{2,1,0:T(8,128)(2,1)S(1)}, bf16[8,192,128]{2,1,0:T(8,128)(2,1)S(1)}, u32[]{:S(2)}, u32[]{:S(2)}) collective-permute-start(bf16[8,192,128]{2,1,0:T(8,128)(2,1)S(1)} %get-tuple-element.56.refs_3_.refs_0_), channel_id=1, source_target_pairs={{0,4},{4,0},{1,5},{5,1},{2,6},{6,2},{3,7},{7,3},{8,12},{12,8},{9,1... | collective-permute-start | bytes 1179656 | tf_op jit(solution)/shard_map/ppermute | solution.py:66
  15.5 26.8 %collective-permute-start.1 = (bf16[8,192,128]{2,1,0:T(8,128)(2,1)S(1)}, bf16[8,192,128]{2,1,0:T(8,128)(2,1)S(1)}, u32[]{:S(2)}, u32[]{:S(2)}) collective-permute-start(bf16[8,192,128]{2,1,0:T(8,128)(2,1)S(1)} %get-tuple-element.56.refs_3_.refs_0_), channel_id=1, source_target_pairs={{0,2},{2,0},{1,3},{3,1},{4,6},{6,4},{5,7},{7,5},{8,10},{10,8},{9,1... | collective-permute-start | bytes 1179656 | tf_op jit(solution)/shard_map/ppermute | solution.py:66
  16.3 26.6 %collective-permute-start.4 = (bf16[8,192,128]{2,1,0:T(8,128)(2,1)S(1)}, bf16[8,192,128]{2,1,0:T(8,128)(2,1)S(1)}, u32[]{:S(2)}, u32[]{:S(2)}) collective-permute-start(bf16[8,192,128]{2,1,0:T(8,128)(2,1)S(1)} %get-tuple-element.56.refs_3_.refs_0_), channel_id=1, source_target_pairs={{0,1},{1,0},{2,3},{3,2},{4,5},{5,4},{6,7},{7,6},{8,9},{9,8},{10,11... | collective-permute-start | bytes 1179656 | tf_op jit(solution)/shard_map/ppermute | solution.py:55
  24.8 18.1 %collective-permute-start.7 = (bf16[8,192,128]{2,1,0:T(8,128)(2,1)S(1)}, bf16[8,192,128]{2,1,0:T(8,128)(2,1)S(1)}, u32[]{:S(2)}, u32[]{:S(2)}) collective-permute-start(bf16[8,192,128]{2,1,0:T(8,128)(2,1)S(1)} %collective-permute-done.3.refs_6_), channel_id=1, source_target_pairs={{0,1},{1,0},{2,3},{3,2},{4,5},{5,4},{6,7},{7,6},{8,9},{9,8},{10,11... | collective-permute-start | bytes 1179656 | tf_op jit(solution)/shard_map/ppermute | solution.py:55
  51.1 14.4 %collective-permute-start.12 = (bf16[8,96,128]{2,1,0:T(8,128)(2,1)S(1)}, bf16[8,96,128]{2,1,0:T(8,128)(2,1)S(1)}, u32[]{:S(2)}, u32[]{:S(2)}) collective-permute-start(bf16[8,96,128]{2,1,0:T(8,128)(2,1)S(1)} %get-tuple-element.66.refs_3_.refs_1_), channel_id=1, source_target_pairs={{4,8},{8,4},{5,9},{9,5},{6,10},{10,6},{7,11},{11,7},{12,16},{16,12... | collective-permute-start | bytes 589832 | tf_op jit(solution)/shard_map/ppermute | solution.py:66
  52.4 17.7 %collective-permute-start.10 = (bf16[8,96,128]{2,1,0:T(8,128)(2,1)S(1)}, bf16[8,96,128]{2,1,0:T(8,128)(2,1)S(1)}, u32[]{:S(2)}, u32[]{:S(2)}) collective-permute-start(bf16[8,96,128]{2,1,0:T(8,128)(2,1)S(1)} %get-tuple-element.66.refs_3_.refs_1_), channel_id=1, source_target_pairs={{0,4},{4,0},{1,5},{5,1},{2,6},{6,2},{3,7},{7,3},{8,12},{12,8},{9,1... | collective-permute-start | bytes 589832 | tf_op jit(solution)/shard_map/ppermute | solution.py:66
  57.2 14.2 %collective-permute-start.9 = (bf16[8,96,128]{2,1,0:T(8,128)(2,1)S(1)}, bf16[8,96,128]{2,1,0:T(8,128)(2,1)S(1)}, u32[]{:S(2)}, u32[]{:S(2)}) collective-permute-start(bf16[8,96,128]{2,1,0:T(8,128)(2,1)S(1)} %get-tuple-element.66.refs_3_.refs_1_), channel_id=1, source_target_pairs={{0,2},{2,0},{1,3},{3,1},{4,6},{6,4},{5,7},{7,5},{8,10},{10,8},{9,1... | collective-permute-start | bytes 589832 | tf_op jit(solution)/shard_map/ppermute | solution.py:66
  76.5 15.3 %collective-permute-start.21 = (bf16[8,96,128]{2,1,0:T(8,128)(2,1)S(1)}, bf16[8,96,128]{2,1,0:T(8,128)(2,1)S(1)}, u32[]{:S(2)}, u32[]{:S(2)}) collective-permute-start(bf16[8,96,128]{2,1,0:T(8,128)(2,1)S(1)} %get-tuple-element.70.refs_3_.refs_2_), channel_id=1, source_target_pairs={{4,8},{8,4},{5,9},{9,5},{6,10},{10,6},{7,11},{11,7},{12,16},{16,12... | collective-permute-start | bytes 589832 | tf_op jit(solution)/shard_map/ppermute | solution.py:66
  77.2 14.7 %collective-permute-start.20 = (bf16[8,96,128]{2,1,0:T(8,128)(2,1)S(1)}, bf16[8,96,128]{2,1,0:T(8,128)(2,1)S(1)}, u32[]{:S(2)}, u32[]{:S(2)}) collective-permute-start(bf16[8,96,128]{2,1,0:T(8,128)(2,1)S(1)} %get-tuple-element.70.refs_3_.refs_2_), channel_id=1, source_target_pairs={{2,4},{4,2},{3,5},{5,3},{6,8},{8,6},{7,9},{9,7},{10,12},{12,10},{1... | collective-permute-start | bytes 589832 | tf_op jit(solution)/shard_map/ppermute | solution.py:66
  77.8 20.8 %collective-permute-start.19 = (bf16[8,96,128]{2,1,0:T(8,128)(2,1)S(1)}, bf16[8,96,128]{2,1,0:T(8,128)(2,1)S(1)}, u32[]{:S(2)}, u32[]{:S(2)}) collective-permute-start(bf16[8,96,128]{2,1,0:T(8,128)(2,1)S(1)} %get-tuple-element.70.refs_3_.refs_2_), channel_id=1, source_target_pairs={{0,4},{4,0},{1,5},{5,1},{2,6},{6,2},{3,7},{7,3},{8,12},{12,8},{9,1... | collective-permute-start | bytes 589832 | tf_op jit(solution)/shard_map/ppermute | solution.py:66
  85.6 14.2 %collective-permute-start.18 = (bf16[8,96,128]{2,1,0:T(8,128)(2,1)S(1)}, bf16[8,96,128]{2,1,0:T(8,128)(2,1)S(1)}, u32[]{:S(2)}, u32[]{:S(2)}) collective-permute-start(bf16[8,96,128]{2,1,0:T(8,128)(2,1)S(1)} %get-tuple-element.70.refs_3_.refs_2_), channel_id=1, source_target_pairs={{0,2},{2,0},{1,3},{3,1},{4,6},{6,4},{5,7},{7,5},{8,10},{10,8},{9,1... | collective-permute-start | bytes 589832 | tf_op jit(solution)/shard_map/ppermute | solution.py:66
  104.9 14.4 %collective-permute-start.30 = (bf16[8,96,128]{2,1,0:T(8,128)(2,1)S(1)}, bf16[8,96,128]{2,1,0:T(8,128)(2,1)S(1)}, u32[]{:S(2)}, u32[]{:S(2)}) collective-permute-start(bf16[8,96,128]{2,1,0:T(8,128)(2,1)S(1)} %get-tuple-element.74.refs_3_), channel_id=1, source_target_pairs={{4,8},{8,4},{5,9},{9,5},{6,10},{10,6},{7,11},{11,7},{12,16},{16,12... | collective-permute-start | bytes 589832 | tf_op jit(solution)/shard_map/ppermute | solution.py:66
  106.2 18.4 %collective-permute-start.28 = (bf16[8,96,128]{2,1,0:T(8,128)(2,1)S(1)}, bf16[8,96,128]{2,1,0:T(8,128)(2,1)S(1)}, u32[]{:S(2)}, u32[]{:S(2)}) collective-permute-start(bf16[8,96,128]{2,1,0:T(8,128)(2,1)S(1)} %get-tuple-element.74.refs_3_), channel_id=1, source_target_pairs={{0,4},{4,0},{1,5},{5,1},{2,6},{6,2},{3,7},{7,3},{8,12},{12,8},{9,1... | collective-permute-start | bytes 589832 | tf_op jit(solution)/shard_map/ppermute | solution.py:66
  111.5 14.2 %collective-permute-start.27 = (bf16[8,96,128]{2,1,0:T(8,128)(2,1)S(1)}, bf16[8,96,128]{2,1,0:T(8,128)(2,1)S(1)}, u32[]{:S(2)}, u32[]{:S(2)}) collective-permute-start(bf16[8,96,128]{2,1,0:T(8,128)(2,1)S(1)} %get-tuple-element.74.refs_3_), channel_id=1, source_target_pairs={{0,2},{2,0},{1,3},{3,1},{4,6},{6,4},{5,7},{7,5},{8,10},{10,8},{9,1... | collective-permute-start | bytes 589832 | tf_op jit(solution)/shard_map/ppermute | solution.py:66
  130.8 15.0 %collective-permute-start.39 = (bf16[8,96,128]{2,1,0:T(8,128)(2,1)S(1)}, bf16[8,96,128]{2,1,0:T(8,128)(2,1)S(1)}, u32[]{:S(2)}, u32[]{:S(2)}) collective-permute-start(bf16[8,96,128]{2,1,0:T(8,128)(2,1)S(1)} %get-tuple-element.78.refs_3_.refs_4_), channel_id=1, source_target_pairs={{4,8},{8,4},{5,9},{9,5},{6,10},{10,6},{7,11},{11,7},{12,16},{16,12... | collective-permute-start | bytes 589832 | tf_op jit(solution)/shard_map/ppermute | solution.py:66
  131.5 14.4 %collective-permute-start.38 = (bf16[8,96,128]{2,1,0:T(8,128)(2,1)S(1)}, bf16[8,96,128]{2,1,0:T(8,128)(2,1)S(1)}, u32[]{:S(2)}, u32[]{:S(2)}) collective-permute-start(bf16[8,96,128]{2,1,0:T(8,128)(2,1)S(1)} %get-tuple-element.78.refs_3_.refs_4_), channel_id=1, source_target_pairs={{2,4},{4,2},{3,5},{5,3},{6,8},{8,6},{7,9},{9,7},{10,12},{12,10},{1... | collective-permute-start | bytes 589832 | tf_op jit(solution)/shard_map/ppermute | solution.py:66
  132.2 20.2 %collective-permute-start.37 = (bf16[8,96,128]{2,1,0:T(8,128)(2,1)S(1)}, bf16[8,96,128]{2,1,0:T(8,128)(2,1)S(1)}, u32[]{:S(2)}, u32[]{:S(2)}) collective-permute-start(bf16[8,96,128]{2,1,0:T(8,128)(2,1)S(1)} %get-tuple-element.78.refs_3_.refs_4_), channel_id=1, source_target_pairs={{0,4},{4,0},{1,5},{5,1},{2,6},{6,2},{3,7},{7,3},{8,12},{12,8},{9,1... | collective-permute-start | bytes 589832 | tf_op jit(solution)/shard_map/ppermute | solution.py:66
  139.4 14.2 %collective-permute-start.36 = (bf16[8,96,128]{2,1,0:T(8,128)(2,1)S(1)}, bf16[8,96,128]{2,1,0:T(8,128)(2,1)S(1)}, u32[]{:S(2)}, u32[]{:S(2)}) collective-permute-start(bf16[8,96,128]{2,1,0:T(8,128)(2,1)S(1)} %get-tuple-element.78.refs_3_.refs_4_), channel_id=1, source_target_pairs={{0,2},{2,0},{1,3},{3,1},{4,6},{6,4},{5,7},{7,5},{8,10},{10,8},{9,1... | collective-permute-start | bytes 589832 | tf_op jit(solution)/shard_map/ppermute | solution.py:66
  141.2 21.5 %collective-permute-start.40 = (bf16[8,96,128]{2,1,0:T(8,128)(2,1)S(1)}, bf16[8,96,128]{2,1,0:T(8,128)(2,1)S(1)}, u32[]{:S(2)}, u32[]{:S(2)}) collective-permute-start(bf16[8,96,128]{2,1,0:T(8,128)(2,1)S(1)} %get-tuple-element.78.refs_3_.refs_4_), channel_id=1, source_target_pairs={{0,1},{1,0},{2,3},{3,2},{4,5},{5,4},{6,7},{7,6},{8,9},{9,8},{10,11... | collective-permute-start | bytes 589832 | tf_op jit(solution)/shard_map/ppermute | solution.py:55
  145.9 16.8 %collective-permute-start.43 = (bf16[8,96,128]{2,1,0:T(8,128)(2,1)S(1)}, bf16[8,96,128]{2,1,0:T(8,128)(2,1)S(1)}, u32[]{:S(2)}, u32[]{:S(2)}) collective-permute-start(bf16[8,96,128]{2,1,0:T(8,128)(2,1)S(1)} %collective-permute-done.38.refs_6_), channel_id=1, source_target_pairs={{0,1},{1,0},{2,3},{3,2},{4,5},{5,4},{6,7},{7,6},{8,9},{9,8},{10,11... | collective-permute-start | bytes 589832 | tf_op jit(solution)/shard_map/ppermute | solution.py:55
  167.3 15.0 %collective-permute-start.48 = (bf16[8,96,128]{2,1,0:T(8,128)(2,1)S(1)}, bf16[8,96,128]{2,1,0:T(8,128)(2,1)S(1)}, u32[]{:S(2)}, u32[]{:S(2)}) collective-permute-start(bf16[8,96,128]{2,1,0:T(8,128)(2,1)S(1)} %get-tuple-element.82.refs_3_.refs_5_), channel_id=1, source_target_pairs={{4,8},{8,4},{5,9},{9,5},{6,10},{10,6},{7,11},{11,7},{12,16},{16,12... | collective-permute-start | bytes 589832 | tf_op jit(solution)/shard_map/ppermute | solution.py:66
  168.0 14.4 %collective-permute-start.47 = (bf16[8,96,128]{2,1,0:T(8,128)(2,1)S(1)}, bf16[8,96,128]{2,1,0:T(8,128)(2,1)S(1)}, u32[]{:S(2)}, u32[]{:S(2)}) collective-permute-start(bf16[8,96,128]{2,1,0:T(8,128)(2,1)S(1)} %get-tuple-element.82.refs_3_.refs_5_), channel_id=1, source_target_pairs={{2,4},{4,2},{3,5},{5,3},{6,8},{8,6},{7,9},{9,7},{10,12},{12,10},{1... | collective-permute-start | bytes 589832 | tf_op jit(solution)/shard_map/ppermute | solution.py:66
  168.7 16.1 %collective-permute-start.46 = (bf16[8,96,128]{2,1,0:T(8,128)(2,1)S(1)}, bf16[8,96,128]{2,1,0:T(8,128)(2,1)S(1)}, u32[]{:S(2)}, u32[]{:S(2)}) collective-permute-start(bf16[8,96,128]{2,1,0:T(8,128)(2,1)S(1)} %get-tuple-element.82.refs_3_.refs_5_), channel_id=1, source_target_pairs={{0,4},{4,0},{1,5},{5,1},{2,6},{6,2},{3,7},{7,3},{8,12},{12,8},{9,1... | collective-permute-start | bytes 589832 | tf_op jit(solution)/shard_map/ppermute | solution.py:66
  173.9 14.2 %collective-permute-start.45 = (bf16[8,96,128]{2,1,0:T(8,128)(2,1)S(1)}, bf16[8,96,128]{2,1,0:T(8,128)(2,1)S(1)}, u32[]{:S(2)}, u32[]{:S(2)}) collective-permute-start(bf16[8,96,128]{2,1,0:T(8,128)(2,1)S(1)} %get-tuple-element.82.refs_3_.refs_5_), channel_id=1, source_target_pairs={{0,2},{2,0},{1,3},{3,1},{4,6},{6,4},{5,7},{7,5},{8,10},{10,8},{9,1... | collective-permute-start | bytes 589832 | tf_op jit(solution)/shard_map/ppermute | solution.py:66
  193.2 16.2 %collective-permute-start.57 = (bf16[8,96,128]{2,1,0:T(8,128)(2,1)S(1)}, bf16[8,96,128]{2,1,0:T(8,128)(2,1)S(1)}, u32[]{:S(2)}, u32[]{:S(2)}) collective-permute-start(bf16[8,96,128]{2,1,0:T(8,128)(2,1)S(1)} %get-tuple-element.86.refs_3_.refs_6_), channel_id=1, source_target_pairs={{4,8},{8,4},{5,9},{9,5},{6,10},{10,6},{7,11},{11,7},{12,16},{16,12... | collective-permute-start | bytes 589832 | tf_op jit(solution)/shard_map/ppermute | solution.py:66
  193.9 15.6 %collective-permute-start.56 = (bf16[8,96,128]{2,1,0:T(8,128)(2,1)S(1)}, bf16[8,96,128]{2,1,0:T(8,128)(2,1)S(1)}, u32[]{:S(2)}, u32[]{:S(2)}) collective-permute-start(bf16[8,96,128]{2,1,0:T(8,128)(2,1)S(1)} %get-tuple-element.86.refs_3_.refs_6_), channel_id=1, source_target_pairs={{2,4},{4,2},{3,5},{5,3},{6,8},{8,6},{7,9},{9,7},{10,12},{12,10},{1... | collective-permute-start | bytes 589832 | tf_op jit(solution)/shard_map/ppermute | solution.py:66
  194.6 20.2 %collective-permute-start.55 = (bf16[8,96,128]{2,1,0:T(8,128)(2,1)S(1)}, bf16[8,96,128]{2,1,0:T(8,128)(2,1)S(1)}, u32[]{:S(2)}, u32[]{:S(2)}) collective-permute-start(bf16[8,96,128]{2,1,0:T(8,128)(2,1)S(1)} %get-tuple-element.86.refs_3_.refs_6_), channel_id=1, source_target_pairs={{0,4},{4,0},{1,5},{5,1},{2,6},{6,2},{3,7},{7,3},{8,12},{12,8},{9,1... | collective-permute-start | bytes 589832 | tf_op jit(solution)/shard_map/ppermute | solution.py:66
  201.8 14.2 %collective-permute-start.54 = (bf16[8,96,128]{2,1,0:T(8,128)(2,1)S(1)}, bf16[8,96,128]{2,1,0:T(8,128)(2,1)S(1)}, u32[]{:S(2)}, u32[]{:S(2)}) collective-permute-start(bf16[8,96,128]{2,1,0:T(8,128)(2,1)S(1)} %get-tuple-element.86.refs_3_.refs_6_), channel_id=1, source_target_pairs={{0,2},{2,0},{1,3},{3,1},{4,6},{6,4},{5,7},{7,5},{8,10},{10,8},{9,1... | collective-permute-start | bytes 589832 | tf_op jit(solution)/shard_map/ppermute | solution.py:66
  221.4 16.2 %collective-permute-start.67 = (bf16[8,32,128]{2,1,0:T(8,128)(2,1)S(1)}, bf16[8,32,128]{2,1,0:T(8,128)(2,1)S(1)}, u32[]{:S(2)}, u32[]{:S(2)}) collective-permute-start(bf16[8,32,128]{2,1,0:T(8,128)(2,1)S(1)} %get-tuple-element.98.refs_3_), channel_id=1, source_target_pairs={{0,1},{1,0},{2,3},{3,2},{4,5},{5,4},{6,7},{7,6},{8,9},{9,8},{10,11... | collective-permute-start | bytes 196616 | tf_op jit(solution)/shard_map/ppermute | solution.py:55
  254.8 14.3 %all-to-all-start.1 = ((bf16[32,16,128]{2,1,0:T(8,128)(2,1)}), bf16[32,16,128]{2,1,0:T(8,128)(2,1)S(1)}, u32[]{:S(2)}, u32[]{:S(2)}) async-start(bf16[32,16,128]{2,1,0:T(8,128)(2,1)} %shard_map.135), calls=%async_computation.1 | async-start | bytes 262144 | tf_op jit(solution)/shard_map/all_to_all | solution.py:494
  (45 other events, 242.6 us)
where the time goes:
time: 308 us; the launch traced here: 303 us
  starting transfers between devices  128 us (42%)
  Pallas kernels  69.7 us (23%)
  waiting for transfers between devices  67.8 us (22%)
  blocking collectives  32.7 us (11%)
  local copies, waits for them, and re-layouts  3.8 us (1%)
    ppermute x32, starting transfers between devices, paired(): return lax.ppermute(value, 'blk', pairs)  85.8 us
    pallas_call x19, Pallas kernels, call(): pl.pallas_call(kernel, grid=(1,) if fetch else (), out_shape=out_shape, i...  64.8 us
    ppermute x32, waiting for transfers between devices, paired(): return lax.ppermute(value, 'blk', pairs)  46.5 us
    ppermute x41, starting transfers between devices, swap_cores(): return lax.ppermute(value, 'blk', [(i, i ^ 1) for i in range(n)])  36.8 us
    all_to_all x1, blocking collectives, on_device(): halves = lax.all_to_all(halves, 'region', 0, 0, tiled=True)  20.1 us
    all_to_all x1, blocking collectives, on_device(): lax.all_to_all(packed.reshape(ring, 512 // ring, 2 * rank), 'blk', 0, 0,...  12.6 us
    ppermute x41, waiting for transfers between devices, swap_cores(): return lax.ppermute(value, 'blk', [(i, i ^ 1) for i in range(n)])  12.3 us
    all_to_all x1, waiting for transfers between devices, on_device(): sums = lax.all_to_all(sums, 'blk', 0, 0, tiled=True).reshape(512, 2 * rank)  9.07 us
  transfers between devices with their start and end apart: 74, of which 33 were waited for; matrix products, arithmetic and copies ran while one was open for 0% of the time, Pallas kernels for 10%

commit v1 on v0

--- a/solution.py
+++ b/solution.py
@@ -66,17 +66,23 @@
     return lax.ppermute(value, "blk", pairs)
 
 
-def window(value, after=None):
-    direct = [
-        value,
-        paired(value, lambda c: c % 2 == 0, 1),
-        paired(value, lambda c: c % 4 < 2, 2),
-        paired(value, lambda c: c % 2 == 1, 1),
-        paired(value, lambda c: c % 4 >= 2, 2),
-    ]
-    if after is not None:
-        direct[-1], after = lax.optimization_barrier((direct[-1], after))
-    return direct + [swap_cores(v) for v in direct], after
+def even_pairs(value):
+    return paired(value, lambda c: c % 2 == 0, 1)
+
+
+def odd_pairs(value):
+    return paired(value, lambda c: c % 2 == 1, 1)
+
+
+def window(value, beside):
+    other = odd_pairs(value)
+    near = even_pairs(value)
+    other, made = beside(other)
+    passed = odd_pairs(near)
+    last = even_pairs(other)
+    last, made = lax.optimization_barrier((last, made))
+    direct = [value, near, other, last, passed]
+    return direct + [swap_cores(v) for v in direct], made
 
 
 def index_kernel(device_ref, cols_ref, delay_ref, slot_ref, *refs):
@@ -109,8 +115,7 @@
         list_ref[spot + i] = top + 1
     list_ref[list_ref.shape[0] - 1] = (spot + 2 * TOGETHER - 1) // (2 * TOGETHER)
     odd = jnp.where(chip % 2 == 0, 1, -1)
-    two = jnp.where(chip % 4 < 2, 2, -2)
-    for i, rel in enumerate((0, odd, two, -odd, -two)):
+    for i, rel in enumerate((0, odd, -odd, 2 * odd, -2 * odd)):
         off_ref[i] = ((rel + SPAN) * 2 + core) * blocks
         off_ref[i + 5] = ((rel + SPAN) * 2 + 1 - core) * blocks
     for copy in copies:
@@ -439,17 +444,22 @@
         packs = len(moms) if n == steps - 2 else 0
         tail, aliases, scratch = [], {}, []
         if n == 0:
-            pieces, code = window(payload, code)
+            pieces, code = window(payload, lambda arrived: (arrived, code))
         else:
             wide = pulses if last else held
-            early = call(
-                functools.partial(early_kernel, n),
-                shape((blocks, wide, rows), F32),
-                [in_vmem(tiles), in_vmem(hist)],
-                [code],
-                flops=flops,
-            )
-            pieces, early = window(payload, early)
+
+            def beside(arrived):
+                arrived, codes = lax.optimization_barrier((arrived, code))
+                early = call(
+                    functools.partial(early_kernel, n),
+                    shape((blocks, wide, rows), F32),
+                    [in_vmem(tiles), in_vmem(hist)],
+                    [codes],
+                    flops=flops,
+                )
+                return arrived, early
+
+            pieces, early = window(payload, beside)
             tail = [in_vmem(hist), early]
             scratch = [pltpu.VMEM((blocks, wide, rows), F32)]
         args = pieces + [in_vmem(tiles), inc, sinv, fout] + tail

time: 308 us -> 300 us (0.974)
  waiting for transfers between devices: 67.8 us -> 21.6 us
  starting transfers between devices: 128 us -> 155 us
  blocking collectives: 32.7 us -> 46.9 us
    ppermute x32, waiting for transfers between devices: 46.5 us -> 0.08 us  [paired(): return lax.ppermute(value, 'blk', pairs)]
    ppermute x32, starting transfers between devices: 85.8 us -> 121 us  [paired(): return lax.ppermute(value, 'blk', pairs)]
    all_to_all x1, blocking collectives: 12.6 us -> 25.9 us  [on_device(): lax.all_to_all(packed.reshape(ring, 512 // ring, 2 * rank), 'blk', 0, 0,...]
    ppermute x41, starting transfers between devices: 36.8 us -> 28.4 us  [swap_cores(): return lax.ppermute(value, 'blk', [(i, i ^ 1) for i in range(n)])]
  transfers between devices with their start and end apart: 74 -> 74, of which waited for: 33 -> 20; matrix products, arithmetic and copies ran while one was open for 0% -> 0% of each run, Pallas kernels for 10% -> 10%
where the time goes in v1:
time: 300 us; the launch traced here: 296 us
  starting transfers between devices  155 us (52%)
  Pallas kernels  68.2 us (23%)
  blocking collectives  46.9 us (16%)
  waiting for transfers between devices  21.6 us (7%)
  local copies, waits for them, and re-layouts  3.8 us (1%)
    ppermute x32, starting transfers between devices, paired(): return lax.ppermute(value, 'blk', pairs)  121 us
    pallas_call x19, Pallas kernels, call(): pl.pallas_call(kernel, grid=(1,) if fetch else (), out_shape=out_shape, i...  63.3 us
    ppermute x41, starting transfers between devices, swap_cores(): return lax.ppermute(value, 'blk', [(i, i ^ 1) for i in range(n)])  28.4 us
    all_to_all x1, blocking collectives, on_device(): lax.all_to_all(packed.reshape(ring, 512 // ring, 2 * rank), 'blk', 0, 0,...  25.9 us
    all_to_all x1, blocking collectives, on_device(): halves = lax.all_to_all(halves, 'region', 0, 0, tiled=True)  21 us
    ppermute x41, waiting for transfers between devices, swap_cores(): return lax.ppermute(value, 'blk', [(i, i ^ 1) for i in range(n)])  12.5 us
    all_to_all x1, waiting for transfers between devices, on_device(): sums = lax.all_to_all(sums, 'blk', 0, 0, tiled=True).reshape(512, 2 * rank)  9.07 us
  transfers between devices with their start and end apart: 74, of which 20 were waited for; matrix products, arithmetic and copies ran while one was open for 0% of the time, Pallas kernels for 10%

profile of v1, /device:TPU:1, one launch (start us, length us, event | category | flops | bytes accessed | tf_op | source)
XLA Modules:
  0.0 296.0 jit_solution(3870360092802139007)
XLA Ops:
  4.3 5.4 %collective-permute-start.2 = (bf16[8,192,128]{2,1,0:T(8,128)(2,1)S(1)}, bf16[8,192,128]{2,1,0:T(8,128)(2,1)S(1)}, u32[]{:S(2)}, u32[]{:S(2)}) collective-permute-start(bf16[8,192,128]{2,1,0:T(8,128)(2,1)S(1)} %get-tuple-element.70.refs_3_.refs_0_), channel_id=1, source_target_pairs={{0,2},{2,0},{1,3},{3,1},{4,6},{6,4},{5,7},{7,5},{8,10},{10,8},{9,1... | collective-permute-start | bytes 1179656 | tf_op jit(solution)/shard_map/ppermute | solution.py:66
  9.7 8.6 %collective-permute-start.1 = (bf16[8,192,128]{2,1,0:T(8,128)(2,1)S(1)}, bf16[8,192,128]{2,1,0:T(8,128)(2,1)S(1)}, u32[]{:S(2)}, u32[]{:S(2)}) collective-permute-start(bf16[8,192,128]{2,1,0:T(8,128)(2,1)S(1)} %collective-permute-done.refs_5_), channel_id=1, source_target_pairs={{0,2},{2,0},{1,3},{3,1},{4,6},{6,4},{5,7},{7,5},{8,10},{10,8},{9,1... | collective-permute-start | bytes 1179656 | tf_op jit(solution)/shard_map/ppermute | solution.py:66
  22.8 4.9 %shard_map.119 = (s32[256]{0:T(256)S(1)}, s32[10]{0:T(128)S(1)}, s32[280]{0:T(512)S(1)}, bf16[8,32,128,128]{3,2,1,0:T(8,128)(2,1)S(1)}, bf16[8,8,32,128]{3,2,1,0...) custom-call(s32[1]{0:T(128)} %bitcast.7.device_ref, s32[8,32]{1,0:T(8,128)S(1)} %bitcast.19, ...), custom_call_target="tpu_custom_call" | custom-call | bytes 16777216 | tf_op jit(solution)/shard_map/pallas_call | solution.py:418
  31.2 6.3 %shard_map.120 = (bf16[324,96,128]{2,1,0:T(8,128)(2,1)S(1)}, bf16[8,96,128]{2,1,0:T(8,128)(2,1)S(1)}, f32[96,64]{1,0:T(8,128)S(1)}) custom-call(s32[256]{0:T(256)S(1)} %get-tuple-element.126.refs_0_.code_ref, s32[10]{0:T(128)S(1)} %get-tuple-element.73.refs_1_, s32[280]{0:T(512)S(1)} %get-tuple-element.74.refs_2_, ...), custom_call_target="tpu_custom_call" | custom-call | flops 805306368 | bytes 1048576 | tf_op jit(solution)/shard_map/pallas_call | solution.py:36
  38.1 8.3 %collective-permute-start.9 = (bf16[8,96,128]{2,1,0:T(8,128)(2,1)S(1)}, bf16[8,96,128]{2,1,0:T(8,128)(2,1)S(1)}, u32[]{:S(2)}, u32[]{:S(2)}) collective-permute-start(bf16[8,96,128]{2,1,0:T(8,128)(2,1)S(1)} %get-tuple-element.80.refs_3_.refs_1_), channel_id=1, source_target_pairs={{0,2},{2,0},{1,3},{3,1},{4,6},{6,4},{5,7},{7,5},{8,10},{10,8},{9,1... | collective-permute-start | bytes 589832 | tf_op jit(solution)/shard_map/ppermute | solution.py:66
  46.4 5.3 %collective-permute-start.11 = (bf16[8,96,128]{2,1,0:T(8,128)(2,1)S(1)}, bf16[8,96,128]{2,1,0:T(8,128)(2,1)S(1)}, u32[]{:S(2)}, u32[]{:S(2)}) collective-permute-start(bf16[8,96,128]{2,1,0:T(8,128)(2,1)S(1)} %collective-permute-done.10.refs_5_), channel_id=1, source_target_pairs={{0,2},{2,0},{1,3},{3,1},{4,6},{6,4},{5,7},{7,5},{8,10},{10,8},{9,1... | collective-permute-start | bytes 589832 | tf_op jit(solution)/shard_map/ppermute | solution.py:66
  54.2 3.6 %shard_map.121.refs_18_ = f32[8,96,128]{2,1,0:T(8,128)S(1)} custom-call(s32[256]{0:T(256)S(1)} %get-tuple-element.126.refs_0_.code_ref, bf16[8,32,128,128]{3,2,1,0:T(8,128)(2,1)S(1)} %get-tuple-element.76.refs_13_.tiles_ref, bf16[324,96,128]{2,1,0:T(8,128)(2,1)S(1)} %get-tuple-element.83.hist_ref.refs_17_), custom_call_target="tpu_custom_call" | custom-call | flops 805306368 | bytes 1048576 | tf_op jit(solution)/shard_map/pallas_call | solution.py:36
  63.5 8.0 %collective-permute-start.18 = (bf16[8,96,128]{2,1,0:T(8,128)(2,1)S(1)}, bf16[8,96,128]{2,1,0:T(8,128)(2,1)S(1)}, u32[]{:S(2)}, u32[]{:S(2)}) collective-permute-start(bf16[8,96,128]{2,1,0:T(8,128)(2,1)S(1)} %get-tuple-element.86.refs_3_.refs_2_), channel_id=1, source_target_pairs={{0,2},{2,0},{1,3},{3,1},{4,6},{6,4},{5,7},{7,5},{8,10},{10,8},{9,1... | collective-permute-start | bytes 589832 | tf_op jit(solution)/shard_map/ppermute | solution.py:66
  71.5 6.5 %collective-permute-start.20 = (bf16[8,96,128]{2,1,0:T(8,128)(2,1)S(1)}, bf16[8,96,128]{2,1,0:T(8,128)(2,1)S(1)}, u32[]{:S(2)}, u32[]{:S(2)}) collective-permute-start(bf16[8,96,128]{2,1,0:T(8,128)(2,1)S(1)} %collective-permute-done.19.refs_5_), channel_id=1, source_target_pairs={{0,2},{2,0},{1,3},{3,1},{4,6},{6,4},{5,7},{7,5},{8,10},{10,8},{9,1... | collective-permute-start | bytes 589832 | tf_op jit(solution)/shard_map/ppermute | solution.py:66
  80.0 3.7 %shard_map.123.refs_18_ = f32[8,96,128]{2,1,0:T(8,128)S(1)} custom-call(s32[256]{0:T(256)S(1)} %get-tuple-element.126.refs_0_.code_ref, bf16[8,32,128,128]{3,2,1,0:T(8,128)(2,1)S(1)} %get-tuple-element.76.refs_13_.tiles_ref, bf16[324,96,128]{2,1,0:T(8,128)(2,1)S(1)} %get-tuple-element.89.hist_ref.refs_17_), custom_call_target="tpu_custom_call" | custom-call | flops 805306368 | bytes 1048576 | tf_op jit(solution)/shard_map/pallas_call | solution.py:36
  85.5 3.2 %shard_map.124 = (bf16[324,96,128]{2,1,0:T(8,128)(2,1)S(1)}, bf16[8,96,128]{2,1,0:T(8,128)(2,1)S(1)}, f32[96,64]{1,0:T(8,128)S(1)}) custom-call(s32[256]{0:T(256)S(1)} %get-tuple-element.126.refs_0_.code_ref, s32[10]{0:T(128)S(1)} %get-tuple-element.73.refs_1_, s32[280]{0:T(512)S(1)} %get-tuple-element.74.refs_2_, ...), custom_call_target="tpu_custom_call", output_to_operand_aliasing={{0}: (17, {})} | custom-call | flops 805306368 | bytes 1048576 | tf_op jit(solution)/shard_map/pallas_call | solution.py:36
  89.3 6.5 %collective-permute-start.27 = (bf16[8,96,128]{2,1,0:T(8,128)(2,1)S(1)}, bf16[8,96,128]{2,1,0:T(8,128)(2,1)S(1)}, u32[]{:S(2)}, u32[]{:S(2)}) collective-permute-start(bf16[8,96,128]{2,1,0:T(8,128)(2,1)S(1)} %get-tuple-element.92.refs_3_), channel_id=1, source_target_pairs={{0,2},{2,0},{1,3},{3,1},{4,6},{6,4},{5,7},{7,5},{8,10},{10,8},{9,1... | collective-permute-start | bytes 589832 | tf_op jit(solution)/shard_map/ppermute | solution.py:66
  95.8 6.3 %collective-permute-start.29 = (bf16[8,96,128]{2,1,0:T(8,128)(2,1)S(1)}, bf16[8,96,128]{2,1,0:T(8,128)(2,1)S(1)}, u32[]{:S(2)}, u32[]{:S(2)}) collective-permute-start(bf16[8,96,128]{2,1,0:T(8,128)(2,1)S(1)} %collective-permute-done.28.refs_5_), channel_id=1, source_target_pairs={{0,2},{2,0},{1,3},{3,1},{4,6},{6,4},{5,7},{7,5},{8,10},{10,8},{9,1... | collective-permute-start | bytes 589832 | tf_op jit(solution)/shard_map/ppermute | solution.py:66
  104.0 3.6 %shard_map.125.refs_18_ = f32[8,96,128]{2,1,0:T(8,128)S(1)} custom-call(s32[256]{0:T(256)S(1)} %get-tuple-element.126.refs_0_.code_ref, bf16[8,32,128,128]{3,2,1,0:T(8,128)(2,1)S(1)} %get-tuple-element.76.refs_13_.tiles_ref, bf16[324,96,128]{2,1,0:T(8,128)(2,1)S(1)} %get-tuple-element.95.hist_ref.refs_17_), custom_call_target="tpu_custom_call" | custom-call | flops 805306368 | bytes 1048576 | tf_op jit(solution)/shard_map/pallas_call | solution.py:36
  113.3 8.2 %collective-permute-start.36 = (bf16[8,96,128]{2,1,0:T(8,128)(2,1)S(1)}, bf16[8,96,128]{2,1,0:T(8,128)(2,1)S(1)}, u32[]{:S(2)}, u32[]{:S(2)}) collective-permute-start(bf16[8,96,128]{2,1,0:T(8,128)(2,1)S(1)} %get-tuple-element.98.refs_3_.refs_4_), channel_id=1, source_target_pairs={{0,2},{2,0},{1,3},{3,1},{4,6},{6,4},{5,7},{7,5},{8,10},{10,8},{9,1... | collective-permute-start | bytes 589832 | tf_op jit(solution)/shard_map/ppermute | solution.py:66
  121.5 5.7 %collective-permute-start.38 = (bf16[8,96,128]{2,1,0:T(8,128)(2,1)S(1)}, bf16[8,96,128]{2,1,0:T(8,128)(2,1)S(1)}, u32[]{:S(2)}, u32[]{:S(2)}) collective-permute-start(bf16[8,96,128]{2,1,0:T(8,128)(2,1)S(1)} %collective-permute-done.37.refs_5_), channel_id=1, source_target_pairs={{0,2},{2,0},{1,3},{3,1},{4,6},{6,4},{5,7},{7,5},{8,10},{10,8},{9,1... | collective-permute-start | bytes 589832 | tf_op jit(solution)/shard_map/ppermute | solution.py:66
  129.3 3.7 %shard_map.127.refs_18_ = f32[8,96,128]{2,1,0:T(8,128)S(1)} custom-call(s32[256]{0:T(256)S(1)} %get-tuple-element.126.refs_0_.code_ref, bf16[8,32,128,128]{3,2,1,0:T(8,128)(2,1)S(1)} %get-tuple-element.76.refs_13_.tiles_ref, bf16[324,96,128]{2,1,0:T(8,128)(2,1)S(1)} %get-tuple-element.101.hist_ref.refs_17_), custom_call_target="tpu_custom_call" | custom-call | flops 805306368 | bytes 1048576 | tf_op jit(solution)/shard_map/pallas_call | solution.py:36
  133.0 9.0 %collective-permute-start.44 = (bf16[8,96,128]{2,1,0:T(8,128)(2,1)S(1)}, bf16[8,96,128]{2,1,0:T(8,128)(2,1)S(1)}, u32[]{:S(2)}, u32[]{:S(2)}) collective-permute-start(bf16[8,96,128]{2,1,0:T(8,128)(2,1)S(1)} %collective-permute-done.39.refs_7_), channel_id=1, source_target_pairs={{0,1},{1,0},{2,3},{3,2},{4,5},{5,4},{6,7},{7,6},{8,9},{9,8},{10,11... | collective-permute-start | bytes 589832 | tf_op jit(solution)/shard_map/ppermute | solution.py:55
  143.6 3.2 %shard_map.128 = (bf16[324,96,128]{2,1,0:T(8,128)(2,1)S(1)}, bf16[8,96,128]{2,1,0:T(8,128)(2,1)S(1)}, f32[96,64]{1,0:T(8,128)S(1)}) custom-call(s32[256]{0:T(256)S(1)} %get-tuple-element.126.refs_0_.code_ref, s32[10]{0:T(128)S(1)} %get-tuple-element.73.refs_1_, s32[280]{0:T(512)S(1)} %get-tuple-element.74.refs_2_, ...), custom_call_target="tpu_custom_call", output_to_operand_aliasing={{0}: (17, {})} | custom-call | flops 805306368 | bytes 1048576 | tf_op jit(solution)/shard_map/pallas_call | solution.py:36
  147.4 8.7 %collective-permute-start.45 = (bf16[8,96,128]{2,1,0:T(8,128)(2,1)S(1)}, bf16[8,96,128]{2,1,0:T(8,128)(2,1)S(1)}, u32[]{:S(2)}, u32[]{:S(2)}) collective-permute-start(bf16[8,96,128]{2,1,0:T(8,128)(2,1)S(1)} %get-tuple-element.104.refs_3_.refs_5_), channel_id=1, source_target_pairs={{0,2},{2,0},{1,3},{3,1},{4,6},{6,4},{5,7},{7,5},{8,10},{10,8},{9,1... | collective-permute-start | bytes 589832 | tf_op jit(solution)/shard_map/ppermute | solution.py:66
  156.1 6.0 %collective-permute-start.47 = (bf16[8,96,128]{2,1,0:T(8,128)(2,1)S(1)}, bf16[8,96,128]{2,1,0:T(8,128)(2,1)S(1)}, u32[]{:S(2)}, u32[]{:S(2)}) collective-permute-start(bf16[8,96,128]{2,1,0:T(8,128)(2,1)S(1)} %collective-permute-done.46.refs_5_), channel_id=1, source_target_pairs={{0,2},{2,0},{1,3},{3,1},{4,6},{6,4},{5,7},{7,5},{8,10},{10,8},{9,1... | collective-permute-start | bytes 589832 | tf_op jit(solution)/shard_map/ppermute | solution.py:66
  164.0 3.6 %shard_map.129.refs_18_ = f32[8,96,128]{2,1,0:T(8,128)S(1)} custom-call(s32[256]{0:T(256)S(1)} %get-tuple-element.126.refs_0_.code_ref, bf16[8,32,128,128]{3,2,1,0:T(8,128)(2,1)S(1)} %get-tuple-element.76.refs_13_.tiles_ref, bf16[324,96,128]{2,1,0:T(8,128)(2,1)S(1)} %get-tuple-element.107.hist_ref.refs_17_), custom_call_target="tpu_custom_call" | custom-call | flops 805306368 | bytes 1048576 | tf_op jit(solution)/shard_map/pallas_call | solution.py:36
  173.3 9.2 %collective-permute-start.54 = (bf16[8,96,128]{2,1,0:T(8,128)(2,1)S(1)}, bf16[8,96,128]{2,1,0:T(8,128)(2,1)S(1)}, u32[]{:S(2)}, u32[]{:S(2)}) collective-permute-start(bf16[8,96,128]{2,1,0:T(8,128)(2,1)S(1)} %get-tuple-element.110.refs_3_.refs_6_), channel_id=1, source_target_pairs={{0,2},{2,0},{1,3},{3,1},{4,6},{6,4},{5,7},{7,5},{8,10},{10,8},{9,1... | collective-permute-start | bytes 589832 | tf_op jit(solution)/shard_map/ppermute | solution.py:66
  182.6 5.8 %collective-permute-start.56 = (bf16[8,96,128]{2,1,0:T(8,128)(2,1)S(1)}, bf16[8,96,128]{2,1,0:T(8,128)(2,1)S(1)}, u32[]{:S(2)}, u32[]{:S(2)}) collective-permute-start(bf16[8,96,128]{2,1,0:T(8,128)(2,1)S(1)} %collective-permute-done.55.refs_5_), channel_id=1, source_target_pairs={{0,2},{2,0},{1,3},{3,1},{4,6},{6,4},{5,7},{7,5},{8,10},{10,8},{9,1... | collective-permute-start | bytes 589832 | tf_op jit(solution)/shard_map/ppermute | solution.py:66
  190.4 3.7 %shard_map.131.refs_18_ = f32[8,96,128]{2,1,0:T(8,128)S(1)} custom-call(s32[256]{0:T(256)S(1)} %get-tuple-element.126.refs_0_.code_ref, bf16[8,32,128,128]{3,2,1,0:T(8,128)(2,1)S(1)} %get-tuple-element.76.refs_13_.tiles_ref, bf16[324,96,128]{2,1,0:T(8,128)(2,1)S(1)} %get-tuple-element.113.hist_ref.refs_17_), custom_call_target="tpu_custom_call" | custom-call | flops 805306368 | bytes 1048576 | tf_op jit(solution)/shard_map/pallas_call | solution.py:36
  195.9 3.4 %shard_map.132 = (bf16[324,96,128]{2,1,0:T(8,128)(2,1)S(1)}, bf16[8,96,128]{2,1,0:T(8,128)(2,1)S(1)}, bf16[512,128]{1,0:T(8,128)(2,1)S(1)}, bf16[8,32,128]{2,1,0:T(8,128)(2,1)S(1)}) custom-call(s32[256]{0:T(256)S(1)} %get-tuple-element.126.refs_0_.code_ref, s32[10]{0:T(128)S(1)} %get-tuple-element.73.refs_1_, ...), custom_call_target="tpu_custom_call", output_to_operand_aliasing={{0}: (17, {})} | custom-call | flops 805306368 | bytes 1048576 | tf_op jit(solution)/shard_map/pallas_call | solution.py:36
  200.0 9.7 %collective-permute-start.63 = (bf16[8,32,128]{2,1,0:T(8,128)(2,1)S(1)}, bf16[8,32,128]{2,1,0:T(8,128)(2,1)S(1)}, u32[]{:S(2)}, u32[]{:S(2)}) collective-permute-start(bf16[8,32,128]{2,1,0:T(8,128)(2,1)S(1)} %get-tuple-element.124.refs_3_), channel_id=1, source_target_pairs={{0,2},{2,0},{1,3},{3,1},{4,6},{6,4},{5,7},{7,5},{8,10},{10,8},{9,1... | collective-permute-start | bytes 196616 | tf_op jit(solution)/shard_map/ppermute | solution.py:66
  220.7 25.9 %all_to_all.15.in_ref = bf16[32,16,128]{2,1,0:T(8,128)(2,1)S(1)} all-to-all(bf16[32,16,128]{2,1,0:T(8,128)(2,1)S(1)} %bitcast.18), channel_id=1, replica_groups=mesh['region'=8,'blk'=32] {'blk'}, dimensions={0} | all-to-all | bytes 262144 | tf_op jit(solution)/shard_map/all_to_all | solution.py:502
  247.3 5.1 %all-to-all-start.1 = ((bf16[32,16,128]{2,1,0:T(8,128)(2,1)}), bf16[32,16,128]{2,1,0:T(8,128)(2,1)S(1)}, u32[]{:S(2)}, u32[]{:S(2)}) async-start(bf16[32,16,128]{2,1,0:T(8,128)(2,1)} %shard_map.135), calls=%async_computation.1 | async-start | bytes 262144 | tf_op jit(solution)/shard_map/all_to_all | solution.py:504
  252.5 9.1 %all-to-all-done.1 = bf16[32,16,128]{2,1,0:T(8,128)(2,1)S(1)} async-done(((bf16[32,16,128]{2,1,0:T(8,128)(2,1)}), bf16[32,16,128]{2,1,0:T(8,128)(2,1)S(1)}, u32[]{:S(2)}, u32[]{:S(2)}) %all-to-all-start.1) | async-done | bytes 131104 | tf_op jit(solution)/shard_map/all_to_all | solution.py:504
  262.2 21.0 %all_to_all.16.mine_ref = bf16[8,384,128]{2,1,0:T(8,128)(2,1)S(1)} all-to-all(bf16[8,384,128]{2,1,0:T(8,128)(2,1)S(1)} %shard_map.136), channel_id=1, replica_groups=mesh['region'=8,'blk'=32] {'region'}, dimensions={0} | all-to-all | bytes 1572864 | tf_op jit(solution)/shard_map/all_to_all | solution.py:507
  288.3 7.4 %shard_map.137 = bf16[8,8,32,128]{3,2,1,0:T(8,128)(2,1)} custom-call(s32[2]{0:T(128)S(1)} %pad_add_fusion.place_ref, bf16[8,384,128]{2,1,0:T(8,128)(2,1)S(1)} %all_to_all.16.mine_ref, bf16[8,384,128]{2,1,0:T(8,128)(2,1)S(1)} %collective-permute-done.72.other_ref, bf16[8,192,128]{2,1,0:T(8,128)(2,1)S(1)} %get-tuple-element.70.refs_3_.refs_0_, ...), custom_call_target="tpu_custom_call" | custom-call | bytes 1048576 | tf_op jit(solution)/shard_map/pallas_call | solution.py:36
  (146 shorter events, 66.9 us)
Async XLA Ops:
  4.3 14.0 %collective-permute-start.2 = (bf16[8,192,128]{2,1,0:T(8,128)(2,1)S(1)}, bf16[8,192,128]{2,1,0:T(8,128)(2,1)S(1)}, u32[]{:S(2)}, u32[]{:S(2)}) collective-permute-start(bf16[8,192,128]{2,1,0:T(8,128)(2,1)S(1)} %get-tuple-element.70.refs_3_.refs_0_), channel_id=1, source_target_pairs={{0,2},{2,0},{1,3},{3,1},{4,6},{6,4},{5,7},{7,5},{8,10},{10,8},{9,1... | collective-permute-start | bytes 1179656 | tf_op jit(solution)/shard_map/ppermute | solution.py:66
  9.7 18.6 %collective-permute-start.1 = (bf16[8,192,128]{2,1,0:T(8,128)(2,1)S(1)}, bf16[8,192,128]{2,1,0:T(8,128)(2,1)S(1)}, u32[]{:S(2)}, u32[]{:S(2)}) collective-permute-start(bf16[8,192,128]{2,1,0:T(8,128)(2,1)S(1)} %collective-permute-done.refs_5_), channel_id=1, source_target_pairs={{0,2},{2,0},{1,3},{3,1},{4,6},{6,4},{5,7},{7,5},{8,10},{10,8},{9,1... | collective-permute-start | bytes 1179656 | tf_op jit(solution)/shard_map/ppermute | solution.py:66
  18.3 10.0 %collective-permute-start.3 = (bf16[8,192,128]{2,1,0:T(8,128)(2,1)S(1)}, bf16[8,192,128]{2,1,0:T(8,128)(2,1)S(1)}, u32[]{:S(2)}, u32[]{:S(2)}) collective-permute-start(bf16[8,192,128]{2,1,0:T(8,128)(2,1)S(1)} %collective-permute-done.2.refs_4_), channel_id=1, source_target_pairs={{2,4},{4,2},{3,5},{5,3},{6,8},{8,6},{7,9},{9,7},{10,12},{12,10},{1... | collective-permute-start | bytes 1179656 | tf_op jit(solution)/shard_map/ppermute | solution.py:66
  19.0 9.8 %collective-permute-start.4 = (bf16[8,192,128]{2,1,0:T(8,128)(2,1)S(1)}, bf16[8,192,128]{2,1,0:T(8,128)(2,1)S(1)}, u32[]{:S(2)}, u32[]{:S(2)}) collective-permute-start(bf16[8,192,128]{2,1,0:T(8,128)(2,1)S(1)} %get-tuple-element.70.refs_3_.refs_0_), channel_id=1, source_target_pairs={{0,1},{1,0},{2,3},{3,2},{4,5},{5,4},{6,7},{7,6},{8,9},{9,8},{10,11... | collective-permute-start | bytes 1179656 | tf_op jit(solution)/shard_map/ppermute | solution.py:55
  37.5 9.0 %collective-permute-start.10 = (bf16[8,96,128]{2,1,0:T(8,128)(2,1)S(1)}, bf16[8,96,128]{2,1,0:T(8,128)(2,1)S(1)}, u32[]{:S(2)}, u32[]{:S(2)}) collective-permute-start(bf16[8,96,128]{2,1,0:T(8,128)(2,1)S(1)} %get-tuple-element.80.refs_3_.refs_1_), channel_id=1, source_target_pairs={{2,4},{4,2},{3,5},{5,3},{6,8},{8,6},{7,9},{9,7},{10,12},{12,10},{1... | collective-permute-start | bytes 589832 | tf_op jit(solution)/shard_map/ppermute | solution.py:66
  38.1 13.6 %collective-permute-start.9 = (bf16[8,96,128]{2,1,0:T(8,128)(2,1)S(1)}, bf16[8,96,128]{2,1,0:T(8,128)(2,1)S(1)}, u32[]{:S(2)}, u32[]{:S(2)}) collective-permute-start(bf16[8,96,128]{2,1,0:T(8,128)(2,1)S(1)} %get-tuple-element.80.refs_3_.refs_1_), channel_id=1, source_target_pairs={{0,2},{2,0},{1,3},{3,1},{4,6},{6,4},{5,7},{7,5},{8,10},{10,8},{9,1... | collective-permute-start | bytes 589832 | tf_op jit(solution)/shard_map/ppermute | solution.py:66
  46.4 11.4 %collective-permute-start.11 = (bf16[8,96,128]{2,1,0:T(8,128)(2,1)S(1)}, bf16[8,96,128]{2,1,0:T(8,128)(2,1)S(1)}, u32[]{:S(2)}, u32[]{:S(2)}) collective-permute-start(bf16[8,96,128]{2,1,0:T(8,128)(2,1)S(1)} %collective-permute-done.10.refs_5_), channel_id=1, source_target_pairs={{0,2},{2,0},{1,3},{3,1},{4,6},{6,4},{5,7},{7,5},{8,10},{10,8},{9,1... | collective-permute-start | bytes 589832 | tf_op jit(solution)/shard_map/ppermute | solution.py:66
  51.7 6.2 %collective-permute-start.12 = (bf16[8,96,128]{2,1,0:T(8,128)(2,1)S(1)}, bf16[8,96,128]{2,1,0:T(8,128)(2,1)S(1)}, u32[]{:S(2)}, u32[]{:S(2)}) collective-permute-start(bf16[8,96,128]{2,1,0:T(8,128)(2,1)S(1)} %collective-permute-done.9.refs_4_), channel_id=1, source_target_pairs={{2,4},{4,2},{3,5},{5,3},{6,8},{8,6},{7,9},{9,7},{10,12},{12,10},{1... | collective-permute-start | bytes 589832 | tf_op jit(solution)/shard_map/ppermute | solution.py:66
  62.8 8.6 %collective-permute-start.19 = (bf16[8,96,128]{2,1,0:T(8,128)(2,1)S(1)}, bf16[8,96,128]{2,1,0:T(8,128)(2,1)S(1)}, u32[]{:S(2)}, u32[]{:S(2)}) collective-permute-start(bf16[8,96,128]{2,1,0:T(8,128)(2,1)S(1)} %get-tuple-element.86.refs_3_.refs_2_), channel_id=1, source_target_pairs={{2,4},{4,2},{3,5},{5,3},{6,8},{8,6},{7,9},{9,7},{10,12},{12,10},{1... | collective-permute-start | bytes 589832 | tf_op jit(solution)/shard_map/ppermute | solution.py:66
  63.5 14.5 %collective-permute-start.18 = (bf16[8,96,128]{2,1,0:T(8,128)(2,1)S(1)}, bf16[8,96,128]{2,1,0:T(8,128)(2,1)S(1)}, u32[]{:S(2)}, u32[]{:S(2)}) collective-permute-start(bf16[8,96,128]{2,1,0:T(8,128)(2,1)S(1)} %get-tuple-element.86.refs_3_.refs_2_), channel_id=1, source_target_pairs={{0,2},{2,0},{1,3},{3,1},{4,6},{6,4},{5,7},{7,5},{8,10},{10,8},{9,1... | collective-permute-start | bytes 589832 | tf_op jit(solution)/shard_map/ppermute | solution.py:66
  71.5 12.2 %collective-permute-start.20 = (bf16[8,96,128]{2,1,0:T(8,128)(2,1)S(1)}, bf16[8,96,128]{2,1,0:T(8,128)(2,1)S(1)}, u32[]{:S(2)}, u32[]{:S(2)}) collective-permute-start(bf16[8,96,128]{2,1,0:T(8,128)(2,1)S(1)} %collective-permute-done.19.refs_5_), channel_id=1, source_target_pairs={{0,2},{2,0},{1,3},{3,1},{4,6},{6,4},{5,7},{7,5},{8,10},{10,8},{9,1... | collective-permute-start | bytes 589832 | tf_op jit(solution)/shard_map/ppermute | solution.py:66
  88.6 7.2 %collective-permute-start.28 = (bf16[8,96,128]{2,1,0:T(8,128)(2,1)S(1)}, bf16[8,96,128]{2,1,0:T(8,128)(2,1)S(1)}, u32[]{:S(2)}, u32[]{:S(2)}) collective-permute-start(bf16[8,96,128]{2,1,0:T(8,128)(2,1)S(1)} %get-tuple-element.92.refs_3_), channel_id=1, source_target_pairs={{2,4},{4,2},{3,5},{5,3},{6,8},{8,6},{7,9},{9,7},{10,12},{12,10},{1... | collective-permute-start | bytes 589832 | tf_op jit(solution)/shard_map/ppermute | solution.py:66
  89.3 12.8 %collective-permute-start.27 = (bf16[8,96,128]{2,1,0:T(8,128)(2,1)S(1)}, bf16[8,96,128]{2,1,0:T(8,128)(2,1)S(1)}, u32[]{:S(2)}, u32[]{:S(2)}) collective-permute-start(bf16[8,96,128]{2,1,0:T(8,128)(2,1)S(1)} %get-tuple-element.92.refs_3_), channel_id=1, source_target_pairs={{0,2},{2,0},{1,3},{3,1},{4,6},{6,4},{5,7},{7,5},{8,10},{10,8},{9,1... | collective-permute-start | bytes 589832 | tf_op jit(solution)/shard_map/ppermute | solution.py:66
  95.8 11.9 %collective-permute-start.29 = (bf16[8,96,128]{2,1,0:T(8,128)(2,1)S(1)}, bf16[8,96,128]{2,1,0:T(8,128)(2,1)S(1)}, u32[]{:S(2)}, u32[]{:S(2)}) collective-permute-start(bf16[8,96,128]{2,1,0:T(8,128)(2,1)S(1)} %collective-permute-done.28.refs_5_), channel_id=1, source_target_pairs={{0,2},{2,0},{1,3},{3,1},{4,6},{6,4},{5,7},{7,5},{8,10},{10,8},{9,1... | collective-permute-start | bytes 589832 | tf_op jit(solution)/shard_map/ppermute | solution.py:66
  112.7 8.9 %collective-permute-start.37 = (bf16[8,96,128]{2,1,0:T(8,128)(2,1)S(1)}, bf16[8,96,128]{2,1,0:T(8,128)(2,1)S(1)}, u32[]{:S(2)}, u32[]{:S(2)}) collective-permute-start(bf16[8,96,128]{2,1,0:T(8,128)(2,1)S(1)} %get-tuple-element.98.refs_3_.refs_4_), channel_id=1, source_target_pairs={{2,4},{4,2},{3,5},{5,3},{6,8},{8,6},{7,9},{9,7},{10,12},{12,10},{1... | collective-permute-start | bytes 589832 | tf_op jit(solution)/shard_map/ppermute | solution.py:66
  113.3 13.9 %collective-permute-start.36 = (bf16[8,96,128]{2,1,0:T(8,128)(2,1)S(1)}, bf16[8,96,128]{2,1,0:T(8,128)(2,1)S(1)}, u32[]{:S(2)}, u32[]{:S(2)}) collective-permute-start(bf16[8,96,128]{2,1,0:T(8,128)(2,1)S(1)} %get-tuple-element.98.refs_3_.refs_4_), channel_id=1, source_target_pairs={{0,2},{2,0},{1,3},{3,1},{4,6},{6,4},{5,7},{7,5},{8,10},{10,8},{9,1... | collective-permute-start | bytes 589832 | tf_op jit(solution)/shard_map/ppermute | solution.py:66
  121.5 11.4 %collective-permute-start.38 = (bf16[8,96,128]{2,1,0:T(8,128)(2,1)S(1)}, bf16[8,96,128]{2,1,0:T(8,128)(2,1)S(1)}, u32[]{:S(2)}, u32[]{:S(2)}) collective-permute-start(bf16[8,96,128]{2,1,0:T(8,128)(2,1)S(1)} %collective-permute-done.37.refs_5_), channel_id=1, source_target_pairs={{0,2},{2,0},{1,3},{3,1},{4,6},{6,4},{5,7},{7,5},{8,10},{10,8},{9,1... | collective-permute-start | bytes 589832 | tf_op jit(solution)/shard_map/ppermute | solution.py:66
  127.9 14.4 %collective-permute-start.40 = (bf16[8,96,128]{2,1,0:T(8,128)(2,1)S(1)}, bf16[8,96,128]{2,1,0:T(8,128)(2,1)S(1)}, u32[]{:S(2)}, u32[]{:S(2)}) collective-permute-start(bf16[8,96,128]{2,1,0:T(8,128)(2,1)S(1)} %get-tuple-element.98.refs_3_.refs_4_), channel_id=1, source_target_pairs={{0,1},{1,0},{2,3},{3,2},{4,5},{5,4},{6,7},{7,6},{8,9},{9,8},{10,11... | collective-permute-start | bytes 589832 | tf_op jit(solution)/shard_map/ppermute | solution.py:55
  128.8 13.6 %collective-permute-start.42 = (bf16[8,96,128]{2,1,0:T(8,128)(2,1)S(1)}, bf16[8,96,128]{2,1,0:T(8,128)(2,1)S(1)}, u32[]{:S(2)}, u32[]{:S(2)}) collective-permute-start(bf16[8,96,128]{2,1,0:T(8,128)(2,1)S(1)} %collective-permute-done.37.refs_5_), channel_id=1, source_target_pairs={{0,1},{1,0},{2,3},{3,2},{4,5},{5,4},{6,7},{7,6},{8,9},{9,8},{10,11... | collective-permute-start | bytes 589832 | tf_op jit(solution)/shard_map/ppermute | solution.py:55
  128.9 13.5 %collective-permute-start.41 = (bf16[8,96,128]{2,1,0:T(8,128)(2,1)S(1)}, bf16[8,96,128]{2,1,0:T(8,128)(2,1)S(1)}, u32[]{:S(2)}, u32[]{:S(2)}) collective-permute-start(bf16[8,96,128]{2,1,0:T(8,128)(2,1)S(1)} %collective-permute-done.36.refs_4_), channel_id=1, source_target_pairs={{0,1},{1,0},{2,3},{3,2},{4,5},{5,4},{6,7},{7,6},{8,9},{9,8},{10,11... | collective-permute-start | bytes 589832 | tf_op jit(solution)/shard_map/ppermute | solution.py:55
  133.0 10.3 %collective-permute-start.44 = (bf16[8,96,128]{2,1,0:T(8,128)(2,1)S(1)}, bf16[8,96,128]{2,1,0:T(8,128)(2,1)S(1)}, u32[]{:S(2)}, u32[]{:S(2)}) collective-permute-start(bf16[8,96,128]{2,1,0:T(8,128)(2,1)S(1)} %collective-permute-done.39.refs_7_), channel_id=1, source_target_pairs={{0,1},{1,0},{2,3},{3,2},{4,5},{5,4},{6,7},{7,6},{8,9},{9,8},{10,11... | collective-permute-start | bytes 589832 | tf_op jit(solution)/shard_map/ppermute | solution.py:55
  146.7 9.4 %collective-permute-start.46 = (bf16[8,96,128]{2,1,0:T(8,128)(2,1)S(1)}, bf16[8,96,128]{2,1,0:T(8,128)(2,1)S(1)}, u32[]{:S(2)}, u32[]{:S(2)}) collective-permute-start(bf16[8,96,128]{2,1,0:T(8,128)(2,1)S(1)} %get-tuple-element.104.refs_3_.refs_5_), channel_id=1, source_target_pairs={{2,4},{4,2},{3,5},{5,3},{6,8},{8,6},{7,9},{9,7},{10,12},{12,10},{1... | collective-permute-start | bytes 589832 | tf_op jit(solution)/shard_map/ppermute | solution.py:66
  147.4 14.7 %collective-permute-start.45 = (bf16[8,96,128]{2,1,0:T(8,128)(2,1)S(1)}, bf16[8,96,128]{2,1,0:T(8,128)(2,1)S(1)}, u32[]{:S(2)}, u32[]{:S(2)}) collective-permute-start(bf16[8,96,128]{2,1,0:T(8,128)(2,1)S(1)} %get-tuple-element.104.refs_3_.refs_5_), channel_id=1, source_target_pairs={{0,2},{2,0},{1,3},{3,1},{4,6},{6,4},{5,7},{7,5},{8,10},{10,8},{9,1... | collective-permute-start | bytes 589832 | tf_op jit(solution)/shard_map/ppermute | solution.py:66
  156.1 11.6 %collective-permute-start.47 = (bf16[8,96,128]{2,1,0:T(8,128)(2,1)S(1)}, bf16[8,96,128]{2,1,0:T(8,128)(2,1)S(1)}, u32[]{:S(2)}, u32[]{:S(2)}) collective-permute-start(bf16[8,96,128]{2,1,0:T(8,128)(2,1)S(1)} %collective-permute-done.46.refs_5_), channel_id=1, source_target_pairs={{0,2},{2,0},{1,3},{3,1},{4,6},{6,4},{5,7},{7,5},{8,10},{10,8},{9,1... | collective-permute-start | bytes 589832 | tf_op jit(solution)/shard_map/ppermute | solution.py:66
  172.7 9.9 %collective-permute-start.55 = (bf16[8,96,128]{2,1,0:T(8,128)(2,1)S(1)}, bf16[8,96,128]{2,1,0:T(8,128)(2,1)S(1)}, u32[]{:S(2)}, u32[]{:S(2)}) collective-permute-start(bf16[8,96,128]{2,1,0:T(8,128)(2,1)S(1)} %get-tuple-element.110.refs_3_.refs_6_), channel_id=1, source_target_pairs={{2,4},{4,2},{3,5},{5,3},{6,8},{8,6},{7,9},{9,7},{10,12},{12,10},{1... | collective-permute-start | bytes 589832 | tf_op jit(solution)/shard_map/ppermute | solution.py:66
  173.3 15.1 %collective-permute-start.54 = (bf16[8,96,128]{2,1,0:T(8,128)(2,1)S(1)}, bf16[8,96,128]{2,1,0:T(8,128)(2,1)S(1)}, u32[]{:S(2)}, u32[]{:S(2)}) collective-permute-start(bf16[8,96,128]{2,1,0:T(8,128)(2,1)S(1)} %get-tuple-element.110.refs_3_.refs_6_), channel_id=1, source_target_pairs={{0,2},{2,0},{1,3},{3,1},{4,6},{6,4},{5,7},{7,5},{8,10},{10,8},{9,1... | collective-permute-start | bytes 589832 | tf_op jit(solution)/shard_map/ppermute | solution.py:66
  182.6 11.5 %collective-permute-start.56 = (bf16[8,96,128]{2,1,0:T(8,128)(2,1)S(1)}, bf16[8,96,128]{2,1,0:T(8,128)(2,1)S(1)}, u32[]{:S(2)}, u32[]{:S(2)}) collective-permute-start(bf16[8,96,128]{2,1,0:T(8,128)(2,1)S(1)} %collective-permute-done.55.refs_5_), channel_id=1, source_target_pairs={{0,2},{2,0},{1,3},{3,1},{4,6},{6,4},{5,7},{7,5},{8,10},{10,8},{9,1... | collective-permute-start | bytes 589832 | tf_op jit(solution)/shard_map/ppermute | solution.py:66
  199.3 11.2 %collective-permute-start.64 = (bf16[8,32,128]{2,1,0:T(8,128)(2,1)S(1)}, bf16[8,32,128]{2,1,0:T(8,128)(2,1)S(1)}, u32[]{:S(2)}, u32[]{:S(2)}) collective-permute-start(bf16[8,32,128]{2,1,0:T(8,128)(2,1)S(1)} %get-tuple-element.124.refs_3_), channel_id=1, source_target_pairs={{2,4},{4,2},{3,5},{5,3},{6,8},{8,6},{7,9},{9,7},{10,12},{12,10},{1... | collective-permute-start | bytes 196616 | tf_op jit(solution)/shard_map/ppermute | solution.py:66
  200.0 12.8 %collective-permute-start.63 = (bf16[8,32,128]{2,1,0:T(8,128)(2,1)S(1)}, bf16[8,32,128]{2,1,0:T(8,128)(2,1)S(1)}, u32[]{:S(2)}, u32[]{:S(2)}) collective-permute-start(bf16[8,32,128]{2,1,0:T(8,128)(2,1)S(1)} %get-tuple-element.124.refs_3_), channel_id=1, source_target_pairs={{0,2},{2,0},{1,3},{3,1},{4,6},{6,4},{5,7},{7,5},{8,10},{10,8},{9,1... | collective-permute-start | bytes 196616 | tf_op jit(solution)/shard_map/ppermute | solution.py:66
  209.6 7.6 %collective-permute-start.67 = (bf16[8,32,128]{2,1,0:T(8,128)(2,1)S(1)}, bf16[8,32,128]{2,1,0:T(8,128)(2,1)S(1)}, u32[]{:S(2)}, u32[]{:S(2)}) collective-permute-start(bf16[8,32,128]{2,1,0:T(8,128)(2,1)S(1)} %get-tuple-element.124.refs_3_), channel_id=1, source_target_pairs={{0,1},{1,0},{2,3},{3,2},{4,5},{5,4},{6,7},{7,6},{8,9},{9,8},{10,11... | collective-permute-start | bytes 196616 | tf_op jit(solution)/shard_map/ppermute | solution.py:55
  210.5 6.8 %collective-permute-start.69 = (bf16[8,32,128]{2,1,0:T(8,128)(2,1)S(1)}, bf16[8,32,128]{2,1,0:T(8,128)(2,1)S(1)}, u32[]{:S(2)}, u32[]{:S(2)}) collective-permute-start(bf16[8,32,128]{2,1,0:T(8,128)(2,1)S(1)} %collective-permute-done.64.refs_5_), channel_id=1, source_target_pairs={{0,1},{1,0},{2,3},{3,2},{4,5},{5,4},{6,7},{7,6},{8,9},{9,8},{10,11... | collective-permute-start | bytes 196616 | tf_op jit(solution)/shard_map/ppermute | solution.py:55
  247.3 14.3 %all-to-all-start.1 = ((bf16[32,16,128]{2,1,0:T(8,128)(2,1)}), bf16[32,16,128]{2,1,0:T(8,128)(2,1)S(1)}, u32[]{:S(2)}, u32[]{:S(2)}) async-start(bf16[32,16,128]{2,1,0:T(8,128)(2,1)} %shard_map.135), calls=%async_computation.1 | async-start | bytes 262144 | tf_op jit(solution)/shard_map/all_to_all | solution.py:504
  (45 other events, 160.4 us)
